TPU v7x, 128 devices: a whole 4x4x4 slice. The times are simulated.
128 devices in a mesh: store: 4 (over z), blk: 16 (over x, y), tp: 2 (over core).
Axes of the slice: x: 4, y: 4, z: 4, core: 2. Of those that a mesh axis runs over, the one named last changes fastest.
Arguments:
- queries: bfloat16 [4, 2048, 4096], P('store', 'blk', 'tp'), may hold values from -30 to 30
- suffix_kv: bfloat16 [2, 4, 2048, 512], P(None, 'store', 'blk', 'tp'), may hold values from -4 to 4
- kv_cache: bfloat16 [2, 384, 128, 512], P(None, ('store', 'blk'), 'tp'), may hold values from -4 to 4
- hit_blocks: int32 [4], replicated, may hold values from 8 to 64, as said below
- block_table: int32 [4, 64], replicated, may hold values from 0 to 383, as said below
- dest_slots: int32 [4, 16], replicated, may hold values from 0 to 383, as said below
Outputs:
- attended: bfloat16 [4, 2048, 4096], P('store', 'blk', 'tp')
- cache_out: bfloat16 [2, 384, 128, 512], P(None, ('store', 'blk'), 'tp')
Inputs may be any that keep to these rules, and one draw needn't show every extreme that they name: `hit_blocks`: one request hits exactly 64 blocks, one exactly 8 and one exactly 17; the others between 8 and 32. Slot s lies on the device of store index s // 96 and blk index (s // 6) % 16. All entries are different slots. block_table[r, j] lies on blk index j % 16, and for each request and blk index its 4 blocks of that blk index lie on 4 different store indices. Different slots, none of them in block_table; dest_slots[r, j] lies on blk index (hit_blocks[r] + j) % 16, and the 4 new blocks that go to one blk index lie on 4 different store indices, so each device receives exactly one new block.
All inputs are finite; a program needn't handle non-finite values.
Results may differ from a plain program's by a relative error of at most 0.006.
Values may be sent and summed in bfloat16 or wider, within the bound.
No kernel may reach another device: no remote copies, remote signals or barrier semaphores. Data moves between devices by JAX's collectives and lax.ppermute only.
A program may use at most 128 MiB of HBM per device.

v0:
```python
import functools

import jax
import jax.numpy as jnp
import numpy as np
from jax import lax
from jax.experimental import pallas as pl
from jax.experimental.pallas import tpu as pltpu
from jax.sharding import Mesh, PartitionSpec as P

HD = 128
SUB = 64
TILE = 16
SMALL = 8
ROWS = 1024
MESSAGE = ROWS + 4 * SUB
HALF = 8
NEG_FILL = -1e30
LOG2E = float(np.log2(np.e))
SCALE = HD ** (-0.5) * LOG2E
CAP = 2.0**100
NT = (((1,), (1,)), ((), ()))
TN = (((0,), (0,)), ((), ()))
ANY = pl.BlockSpec(memory_space=pl.ANY)
SMEM = pl.BlockSpec(memory_space=pltpu.SMEM)
VMEM = pl.BlockSpec(memory_space=pltpu.VMEM)
BF16 = jnp.bfloat16
F32 = jnp.float32


def params():
    return pltpu.CompilerParams(vmem_limit_bytes=60 << 20)


def position():
    return tuple(lax.axis_index(n) for n in ("s", "x", "y", "c"))


class Copies:
    def __init__(self, sems):
        self.sems = sems
        self.all = []

    def start(self, src, dst, when=None):
        one = pltpu.make_async_copy(src, dst, self.sems.at[len(self.all)])
        self.all.append((one, when))
        if when is None:
            one.start(priority=1)
        else:
            pl.when(when)(lambda: one.start(priority=1))

    def wait(self):
        for one, when in self.all:
            if when is None:
                one.wait()
            else:
                pl.when(when)(one.wait)


def messages_kernel(queries, suffix, to_a, to_b, q, f, sems):
    _, _, my_y, _ = position()
    copies = Copies(sems)
    copies.start(suffix.at[:, 0], f)
    copies.start(queries.at[0], q)
    copies.wait()
    copies = Copies(sems)
    for order, message in enumerate((to_a, to_b)):
        key_head = (my_y + order) % 2
        for half in range(2):
            cols = pl.ds(pl.multiple_of(key_head * HD, HD), HD)
            rows = pl.ds(half * SUB, SUB)
            for which in range(2):
                at = pl.ds(ROWS + (half * 2 + which) * SUB, SUB)
                copies.start(f.at[which, rows, cols], message.at[at])
        for head in range(8):
            cols = pl.ds(pl.multiple_of(key_head * ROWS + head * HD, HD), HD)
            copies.start(q.at[:, cols], message.at[pl.ds(head * HD, HD)])
    copies.wait()


def make_messages(queries, suffix):
    return pl.pallas_call(
        messages_kernel,
        out_shape=[jax.ShapeDtypeStruct((MESSAGE, HD), BF16)] * 2,
        in_specs=[ANY, ANY],
        out_specs=[ANY] * 2,
        scratch_shapes=[
            pltpu.VMEM(queries.shape[1:], BF16),
            pltpu.VMEM((2,) + suffix.shape[2:], BF16),
            pltpu.SemaphoreType.DMA((24,)),
        ],
        compiler_params=params(),
        name="messages",
    )(queries, suffix)


def pack_kernel(table, cache, after, sent, blocks, sems):
    del after
    my_store, my_x, my_y, _ = position()
    column = my_x * 4 + my_y
    device = my_store * 16 + column
    slots = cache.shape[1]
    copies = Copies(sems)
    for request in range(4):
        slot = jnp.int32(0)
        for turn in range(4):
            entry = table[request, column + 16 * turn]
            slot = jnp.where(entry // slots == device, entry % slots, slot)
        copies.start(cache.at[:, slot], blocks.at[request])
    copies.wait()
    copies = Copies(sems)
    for request in range(4):
        for head in range(4):
            cols = pl.ds(head * HD, HD)
            copies.start(blocks.at[request, :, :, cols], sent.at[request * 4 + head])
    copies.wait()


def pack(table, cache, after):
    return pl.pallas_call(
        pack_kernel,
        out_shape=jax.ShapeDtypeStruct((16, 2, SUB, HD), BF16),
        in_specs=[SMEM, ANY, ANY],
        out_specs=ANY,
        scratch_shapes=[
            pltpu.VMEM((4, 2, SUB, 4 * HD), BF16),
            pltpu.SemaphoreType.DMA((16,)),
        ],
        compiler_params=params(),
        cost_estimate=work(2, 8 * TILE * SUB),
        name="pack",
    )(table, cache, after)


def place_kernel(hits, dests, cache, *refs):
    arrived, out, held, sems = refs[:4], refs[4], refs[5], refs[6]
    my_store, my_x, my_y, _ = position()
    column = my_x * 4 + my_y
    slots = cache.shape[1]
    slot = jnp.int32(0)
    away = jnp.int32(0)
    for k in range(4):
        request = (my_store - k + 4) % 4
        dest = dests[request, (column - hits[request] + 64) % 16]
        here = dest // 96 == my_store
        away = jnp.where(here, k, away)
        slot = jnp.where(here, dest % slots, slot)
    copies = Copies(sems)
    for i in range(slots):
        copies.start(cache.at[:, i], held.at[:, i], when=slot != i)
    for k in range(4):
        copies.start(arrived[k], held.at[:, slot], when=away == k)
    copies.wait()
    copies = Copies(sems)
    copies.start(held, out)
    copies.wait()


def place(hits, dests, cache, arrived):
    return pl.pallas_call(
        place_kernel,
        out_shape=jax.ShapeDtypeStruct(cache.shape, cache.dtype),
        in_specs=[SMEM, SMEM, ANY] + [ANY] * 4,
        out_specs=ANY,
        scratch_shapes=[pltpu.VMEM(cache.shape, BF16), pltpu.SemaphoreType.DMA((10,))],
        compiler_params=params(),
        name="place",
    )(hits, dests, cache, *arrived)


def fold_values(weights, values, rescale, l, acc):
    ones = jnp.ones(values.shape, BF16)
    both = jnp.concatenate([values, ones], axis=1)
    mixed = lax.dot_general(both, weights, TN, preferred_element_type=F32)
    l[0:1, :] = l[0:1, :] * rescale + mixed[HD : HD + 1]
    acc[...] = acc[...] * rescale + mixed[:HD]


def exact_fold(q, keys, values, allowed, m, l, acc):
    scores = lax.dot_general(keys, q, NT, preferred_element_type=F32)
    scores = jnp.where(allowed, scores, NEG_FILL)
    m_old = m[0:1, :]
    m_new = jnp.maximum(m_old, jnp.max(scores, axis=0, keepdims=True) * SCALE)
    weights = jnp.exp2(scores * SCALE - m_new).astype(BF16)
    fold_values(weights, values, jnp.exp2(m_old - m_new), l, acc)
    m[0:1, :] = m_new


def shifted_fold(q, keys, values, allowed, m, l, acc):
    scores = lax.dot_general(keys, q, NT, preferred_element_type=F32)
    weights = jnp.exp2(scores * SCALE - m[0:1, :])
    if allowed is not None:
        weights = jnp.where(allowed, weights, 0.0)
    fold_values(weights.astype(BF16), values, 1.0, l, acc)


def state_shapes(rows):
    return [(rows, 8, ROWS), (rows, 8, ROWS), (rows, HD, ROWS)]


def work(rows, keys):
    units = rows * ROWS * keys
    return pl.CostEstimate(flops=16 * HD * units, bytes_accessed=1 << 21, transcendentals=units)


def keys_at(offset, sources):
    def start(hits, table, refs, fetch, slot):
        my_store, my_x, _, _ = position()
        other_x = (my_x + offset) % 4
        hit_count = hits[my_store]
        step = min(len(sources), 2)

        def both(index, slot):
            if len(sources) <= 2:
                for k, source in enumerate(sources):
                    fetch(refs[source], index, slot + k).start(priority=1)
                return
            for low, pair in ((True, sources[:2]), (False, sources[2:])):
                at = index if low else index - HALF

                @pl.when((index < HALF) if low else (index >= HALF))
                def _(at=at, pair=pair):
                    fetch(refs[pair[0]], at, slot).start(priority=1)
                    fetch(refs[pair[1]], at, slot + 1).start(priority=1)

        for turn in range(4):

            def one(near, slot, turn=turn):
                block = other_x * 4 + near + 16 * turn
                used = block < hit_count

                @pl.when(used)
                def _():
                    both(table[my_store, block] // 96 * 4 + near, slot)

                return jnp.where(used, slot + step, slot)

            slot = lax.fori_loop(0, 4, one, slot)
        return slot

    return start


NEIGHBOURS = (3, 1, 2)


def earlier_rows(sources):
    def start(hits, table, refs, fetch, slot):
        _, my_x, _, _ = position()
        for place, offset in enumerate(NEIGHBOURS):
            earlier = (my_x + offset) % 4 < my_x

            @pl.when(earlier)
            def _(place=place, slot=slot):
                for k, source in enumerate(sources):
                    for part in range(4):
                        at = slot + 4 * k + part
                        fetch(refs[source], 4 * place + part, at).start(priority=1)

            slot = jnp.where(earlier, slot + 8, slot)
        return slot

    return start


def route(hits, sources, held, sems):
    my_store, my_x, my_y, my_core = position()
    own, own_other, rest, rest_other = sources
    for k in range(4):
        near = (my_y + k) % 4
        block = (my_x * 4 + near - hits[my_store] + 64) % 16
        spot = block % 4
        away = (block // 4 - my_x + 4) % 4
        index = 2 * ((spot + my_y) % 2) + my_core
        place = jnp.where(away == 3, 0, away)
        for here in (True, False):
            for same in (True, False):
                source = (own if same else own_other) if here else (rest if same else rest_other)
                at = index if here else 4 * place + index

                @pl.when(((away == 0) == here) & ((spot // 2 == my_core) == same))
                def _(source=source, at=at, k=k):
                    pltpu.make_async_copy(source.at[at], held.at[k], sems.at[k]).start(priority=1)


def attend_kernel(plan, n_sources, chosen, first, last, extra, *refs):
    hits, table = refs[:2]
    sources = refs[2 : 2 + n_sources]
    refs = refs[2 + n_sources :]
    messages = refs[:2]
    rows = len(chosen)
    n_state = 0 if first else 3
    state_in = refs[2 : 2 + n_state]
    refs = refs[2 + n_state :]
    if extra:
        spare = refs[-2:]
        refs = refs[:-2]
    if extra == "route":
        moved, sources = sources[-4:], sources[:-2]
        n_moved = 4
    elif extra == "join":
        moved, sources = sources[-4:], sources[:-4]
        n_moved = 1
    else:
        n_moved = 0
    n_outs = rows if last else 3
    moved_outs = refs[n_outs : n_outs + n_moved]
    refs = refs[:n_outs] + refs[n_outs + n_moved :]
    outs = refs[:n_outs]
    m, l, acc, q, kv, sems, more, stored = refs[n_outs : n_outs + 8]
    refs = refs[n_outs + 8 :]
    state = (m, l, acc)
    _, _, my_y, my_core = position()

    def fetch(source, index, slot):
        start = pl.multiple_of(slot * SUB, SUB)
        return pltpu.make_async_copy(
            source.at[index], kv.at[:, pl.ds(start, SUB), :], sems.at[slot]
        )

    held, held_sems = spare if extra else (None, None)
    loads = Copies(more)
    for i, r in enumerate(chosen):
        loads.start(messages[r].at[pl.ds(0, ROWS)], q.at[i])
    if first:
        near = refs[0]
        for which, source in enumerate(sources):
            owner = my_core if which == 0 else 1 - my_core
            for block in range(2):
                spot = 2 * owner + (my_y + block) % 2
                for half in range(2):
                    at = pl.ds(pl.multiple_of((2 * spot + half) * SUB, SUB), SUB)
                    loads.start(source.at[2 * block + half], near.at[:, at, :])
    else:
        l_old, acc_old = refs[:2]
        for i, r in enumerate(chosen):
            loads.start(state_in[0].at[r], m.at[i])

    count = jnp.int32(0)
    for start in plan:
        count = start(hits, table, sources, fetch, count)

    later = Copies(more.at[pl.ds(len(loads.all), 2 * rows)])
    if not first:
        for i, r in enumerate(chosen):
            later.start(state_in[1].at[r], l_old.at[i])
            later.start(state_in[2].at[r], acc_old.at[i])

    if extra == "route":
        route(hits, (moved[2], moved[3], moved[0], moved[1]), held, held_sems)
    if extra == "join":
        for k in range(4):
            cols = pl.ds(pl.multiple_of((my_y - k + 4) % 4 * HD, HD), HD)
            pltpu.make_async_copy(moved[k], held.at[:, :, cols], held_sems.at[k]).start(priority=1)

    def diagonal(i):
        shape = (8 * SUB, ROWS)
        spot = 2 * my_core + (my_y + i + chosen[0]) % 2
        key_at = lax.broadcasted_iota(jnp.int32, shape, 0)
        row_at = lax.broadcasted_iota(jnp.int32, shape, 1) % HD + spot * HD
        allowed = key_at <= row_at
        exact_fold(q[i], near[0], near[1], allowed, m.at[i], l.at[i], acc.at[i])

    def clear_state(i):
        l[i] = jnp.zeros(l.shape[1:], F32)
        acc[i] = jnp.zeros(acc.shape[1:], F32)

    def wait(slot, _):
        fetch(sources[0], 0, slot).wait()
        return 0

    def tile(i, fold, begin, size, masked):
        start = pl.multiple_of(begin * SUB, SUB)
        keys = kv[0, pl.ds(start, size * SUB), :]
        values = kv[1, pl.ds(start, size * SUB), :]
        allowed = None
        if masked:
            at = lax.broadcasted_iota(jnp.int32, (size * SUB, ROWS), 0)
            allowed = at < (count - begin) * SUB
        fold(q[i], keys, values, allowed, m.at[i], l.at[i], acc.at[i])

    tiles = count // TILE
    done = tiles * TILE
    half = (count - done) // SMALL
    rest = done + half * SMALL

    for i in range(rows):
        clear_state(i)
    loads.wait()

    def one_row(i, _):
        if first:
            m[i] = jnp.full(m.shape[1:], NEG_FILL, F32)
            diagonal(i)

        def arrive(begin, end):
            @pl.when(i == 0)
            def _():
                lax.fori_loop(begin, end, wait, 0)

        def full(t, _):
            arrive(t * TILE, (t + 1) * TILE)
            tile(i, shifted_fold, t * TILE, TILE, False)
            return 0

        lax.fori_loop(0, tiles, full, 0)

        @pl.when(half > 0)
        def _():
            arrive(done, done + SMALL)
            tile(i, shifted_fold, done, SMALL, False)

        @pl.when(rest < count)
        def _():
            arrive(rest, count)

            def clear(slot, _):
                start = pl.multiple_of(slot * SUB, SUB)
                kv[:, pl.ds(start, SUB), :] = jnp.zeros((2, SUB, HD), BF16)
                return 0

            lax.fori_loop(count, rest + SMALL, clear, 0)
            tile(i, shifted_fold, rest, SMALL, True)

        if not first:
            pl.when(i == 0)(later.wait)
            l[i] = l[i] + l_old[i]
            acc[i] = acc[i] + acc_old[i]

        @pl.when(jnp.logical_not(jnp.max(l[i, 0:1, :]) < CAP))
        def _():
            if first:
                m[i] = jnp.full(m.shape[1:], NEG_FILL, F32)
                clear_state(i)
                diagonal(i)
            else:
                l[i] = l_old[i]
                acc[i] = acc_old[i]

            def again(t, _):
                tile(i, exact_fold, t * SMALL, SMALL, True)
                return 0

            lax.fori_loop(0, (count + SMALL - 1) // SMALL, again, 0)

        if last:
            result = acc[i] / l[i, 0:1, :]
            for g in range(8):
                cols = slice(g * HD, (g + 1) * HD)
                refs[2][i, :, cols] = result[:, cols].T.astype(BF16)
        else:
            for k, (here, there) in enumerate(zip(state, outs)):
                pltpu.make_async_copy(here.at[i], there.at[i], stored.at[3 * i + k]).start(
                    priority=1
                )
        return 0

    lax.fori_loop(0, rows, one_row, 0)
    if extra == "route":
        for k in range(4):
            pltpu.make_async_copy(moved[0].at[0], held.at[k], held_sems.at[k]).wait()
        sent = Copies(held_sems)
        for k in range(4):
            sent.start(held.at[k], moved_outs[k])
        sent.wait()
    if extra == "join":
        for k in range(4):
            cols = pl.ds(0, HD)
            pltpu.make_async_copy(moved[k], held.at[:, :, cols], held_sems.at[k]).wait()
        sent = Copies(held_sems)
        sent.start(held, moved_outs[0])
        sent.wait()
    for i in range(rows):
        if last:
            copy = pltpu.make_async_copy(refs[2].at[i], outs[i], stored.at[i])
            copy.start(priority=1)
            copy.wait()
        else:
            for k, (here, there) in enumerate(zip(state, outs)):
                pltpu.make_async_copy(here.at[i], there.at[i], stored.at[3 * i + k]).wait()


def attend(hits, table, plan, most, sources, messages, state, chosen, name, extra=None):
    first = not state
    last = name == "far"
    rows = len(chosen)
    room = max(-(-most // SMALL) * SMALL, SMALL)
    shapes = state_shapes(rows)
    if last:
        out_shape = [jax.ShapeDtypeStruct((HD, ROWS), BF16)] * rows
    else:
        out_shape = [jax.ShapeDtypeStruct(s, F32) for s in shapes]
    scratch = [pltpu.VMEM(s, F32) for s in shapes]
    scratch += [
        pltpu.VMEM((rows, ROWS, HD), BF16),
        pltpu.VMEM((2, room * SUB, HD), BF16),
        pltpu.SemaphoreType.DMA((room,)),
        pltpu.SemaphoreType.DMA(((8 if first else rows) + 3 * rows,)),
        pltpu.SemaphoreType.DMA((3 * rows,)),
    ]
    if first:
        scratch.append(pltpu.VMEM((2, 8 * SUB, HD), BF16))
    else:
        scratch += [pltpu.VMEM(s, F32) for s in shapes[1:]]
    if last:
        scratch.append(pltpu.VMEM((rows, HD, ROWS), BF16))
    if extra == "route":
        out_shape += [jax.ShapeDtypeStruct((2, SUB, HD), BF16)] * 4
        scratch.append(pltpu.VMEM((4, 2, SUB, HD), BF16))
    if extra == "join":
        out_shape += [jax.ShapeDtypeStruct((2, SUB, 4 * HD), BF16)]
        scratch.append(pltpu.VMEM((2, SUB, 4 * HD), BF16))
    if extra:
        scratch.append(pltpu.SemaphoreType.DMA((4,)))
    return pl.pallas_call(
        functools.partial(attend_kernel, plan, len(sources), chosen, first, last, extra),
        out_shape=out_shape,
        in_specs=[SMEM, SMEM] + [ANY] * (len(sources) + 2 + len(state)),
        out_specs=[ANY] * len(out_shape),
        scratch_shapes=scratch,
        compiler_params=params(),
        cost_estimate=work(rows, (most + (8 if first else 0)) * SUB),
        name=name,
    )(hits, table, *sources, *messages, *state)


def by_parity(parity, even, odd):
    return jnp.where(parity == 0, even, odd)


def shift(n, k):
    return [(i, (i + k) % n) for i in range(n)]


def swap(part):
    return lax.ppermute(part, "c", shift(2, 1))


def fresh_part(message):
    return message[ROWS:].reshape(2, 2, SUB, HD)


def shards(queries, suffix_kv, kv_cache, hits, table, dests):
    parity = lax.axis_index("y") % 2
    msg_a, msg_b = make_messages(queries, suffix_kv)
    sent = pack(table, kv_cache, msg_b)
    to_a = [(y * 2 + c, (2 * c + y % 2) * 2 + y // 2) for y in range(4) for c in range(2)]
    to_b = [(y * 2 + c, (2 * c + 1 - y % 2) * 2 + y // 2) for y in range(4) for c in range(2)]
    back_a = [(b, a) for a, b in to_a]
    back_b = [(b, a) for a, b in to_b]
    yc = ("y", "c")
    msg_a = lax.ppermute(msg_a, yc, to_a)
    msg_b = lax.ppermute(msg_b, yc, to_b)
    messages = (msg_a, msg_b)
    fresh = jnp.concatenate([fresh_part(msg_a), fresh_part(msg_b)], axis=0)
    fresh_other = swap(fresh)
    rest = [lax.ppermute(fresh, "x", shift(4, -k)) for k in NEIGHBOURS]
    both = (0, 1)

    def step(state, plan, most, sources, name, extra=None):
        return attend(hits, table, plan, most, sources, messages, state, both, name, extra)

    state = step((), [], 0, (fresh, fresh_other), "diagonal")
    own = lax.all_to_all(sent, ("s", "y"), 0, 0, tiled=True)
    own, state = lax.optimization_barrier((own, state))
    rest = jnp.concatenate(rest, axis=0)
    left = lax.ppermute(own, "x", shift(4, 1))
    right = lax.ppermute(own, "x", shift(4, -1))
    plan = [keys_at(0, (0, 1)), earlier_rows((2, 3))]
    sources = (own, swap(own), rest, swap(rest), fresh, fresh_other)
    *state, p0, p1, p2, p3 = step(state, plan, 56, sources, "own", "route")
    state, left, right, parts = lax.optimization_barrier((state, left, right, (p0, p1, p2, p3)))
    parts = [parts[0]] + [lax.ppermute(parts[k], "y", shift(4, k)) for k in (1, 2, 3)]
    far_a = lax.ppermute(left[:HALF], "x", shift(4, 1))
    far_b = lax.ppermute(right[HALF:], "x", shift(4, -1))
    left_other, right_other = swap(left), swap(right)
    plan = [keys_at(3, (0,)), keys_at(1, (1,))]
    state = step(state, plan, 32, (left, right), "near")
    state, far_a, far_b, parts = lax.optimization_barrier((state, far_a, far_b, parts))
    far = (far_a, swap(far_a), far_b, swap(far_b))
    *state, block = step(state, plan, 32, (left_other, right_other, *parts), "near", "join")
    block, state, far = lax.optimization_barrier((block, state, far))
    arrived = [block] + [lax.ppermute(block, "s", shift(4, k)) for k in (1, 2, 3)]
    plan = [keys_at(2, (0, 1, 2, 3))]
    outs = []
    for r, back in ((0, back_a), (1, back_b)):
        if r == 1:
            arrived, state = lax.optimization_barrier((arrived, state))
        (out,) = attend(hits, table, plan, 32, far, messages, state, (r,), "far")
        outs.append(lax.ppermute(out, yc, back))
    attended = by_parity(
        parity, jnp.concatenate(outs, axis=1), jnp.concatenate(outs[::-1], axis=1)
    )[None]
    cache_out = place(hits, dests, kv_cache, arrived)
    return attended, cache_out


def solution(mesh):
    grid = Mesh(mesh.devices.reshape(4, 4, 4, 2), ("s", "x", "y", "c"))
    blk = ("x", "y")
    return jax.shard_map(
        shards,
        mesh=grid,
        in_specs=(
            P("s", blk, "c"),
            P(None, "s", blk, "c"),
            P(None, ("s", "x", "y"), "c", None),
            P(),
            P(),
            P(),
        ),
        out_specs=(P("s", blk, "c"), P(None, ("s", "x", "y"), "c", None)),
        check_vma=False,
    )
```

profile of v0, /device:TPU:1, one launch (start us, length us, event | category | flops | bytes accessed | tf_op | source)
XLA Modules:
  0.0 119.5 jit_solution(5817442082329717169)
XLA Ops:
  0.6 2.1 %messages.1 = (bf16[1280,128]{1,0:T(8,128)(2,1)}, bf16[1280,128]{1,0:T(8,128)(2,1)}) custom-call(bf16[1,128,2048]{2,1,0:T(8,128)(2,1)} %queries.1, bf16[2,1,128,256]{3,2,1,0:T(8,128)(2,1)} %suffix.1), custom_call_target="tpu_custom_call" | custom-call | tf_op jit(solution)/shard_map/messages/pallas_call | solution.py:82
  2.8 4.2 %collective-permute-start.1 = (bf16[1280,128]{1,0:T(8,128)(2,1)}, bf16[1280,128]{1,0:T(8,128)(2,1)S(1)}, u32[]{:S(2)}, u32[]{:S(2)}) collective-permute-start(bf16[1280,128]{1,0:T(8,128)(2,1)} %get-tuple-element.58.after), channel_id=1, source_target_pairs={{0,2},{1,6},{2,0},{3,4},{4,3},{5,7},{6,1},{7,5},{8,10},{9,14},{10,... | collective-permute-start | bytes 983048 | tf_op jit(solution)/shard_map/ppermute | solution.py:553
  7.0 2.1 %collective-permute-start = (bf16[1280,128]{1,0:T(8,128)(2,1)}, bf16[1280,128]{1,0:T(8,128)(2,1)S(1)}, u32[]{:S(2)}, u32[]{:S(2)}) collective-permute-start(bf16[1280,128]{1,0:T(8,128)(2,1)} %get-tuple-element.59), channel_id=1, source_target_pairs={{0,0},{1,4},{2,2},{3,6},{4,1},{5,5},{6,3},{7,7},{8,8},{9,12},{10,1... | collective-permute-start | bytes 983048 | tf_op jit(solution)/shard_map/ppermute | solution.py:552
  9.1 2.8 %pack.1 = bf16[16,2,64,128]{3,2,1,0:T(8,128)(2,1)} custom-call(s32[4,64]{1,0:T(4,128)} %refs_1_.11, bf16[2,6,64,512]{3,2,1,0:T(8,128)(2,1)} %cache.3, bf16[1280,128]{1,0:T(8,128)(2,1)} %get-tuple-element.58.after), custom_call_target="tpu_custom_call" | custom-call | flops 34359738368 | bytes 2097152 | tf_op jit(solution)/shard_map/pack/pallas_call | solution.py:120
  11.9 5.3 %all-to-all-start = ((bf16[16,2,64,128]{3,2,1,0:T(8,128)(2,1)}), bf16[16,2,64,128]{3,2,1,0:T(8,128)(2,1)S(1)}, u32[]{:S(2)}, u32[]{:S(2)}) async-start(bf16[16,2,64,128]{3,2,1,0:T(8,128)(2,1)} %pack.1), calls=%async_computation | async-start | bytes 1048576 | tf_op jit(solution)/shard_map/all_to_all | solution.py:564
  17.2 3.1 %collective-permute-start.2 = (bf16[4,2,64,128]{3,2,1,0:T(8,128)(2,1)S(1)}, bf16[4,2,64,128]{3,2,1,0:T(8,128)(2,1)S(1)}, u32[]{:S(2)}, u32[]{:S(2)}) collective-permute-start(bf16[4,2,64,128]{3,2,1,0:T(8,128)(2,1)S(1)} %pad_maximum_fusion.refs_2_.refs_6_), channel_id=1, source_target_pairs={{0,1},{1,0},{2,3},{3,2},{4,5},{5,4},{6,7},{7,6},{8,9},{9,8},{10,11... | collective-permute-start | bytes 393224 | tf_op jit(solution)/shard_map/ppermute | solution.py:536
  20.4 1.2 %collective-permute-start.4 = (bf16[4,2,64,128]{3,2,1,0:T(8,128)(2,1)S(1)}, bf16[4,2,64,128]{3,2,1,0:T(8,128)(2,1)S(1)}, u32[]{:S(2)}, u32[]{:S(2)}) collective-permute-start(bf16[4,2,64,128]{3,2,1,0:T(8,128)(2,1)S(1)} %pad_maximum_fusion.refs_2_.refs_6_), channel_id=1, source_target_pairs={{0,8},{8,16},{16,24},{24,0},{1,9},{9,17},{17,25},{25,1},{2,10},{10... | collective-permute-start | bytes 393224 | tf_op jit(solution)/shard_map/ppermute | solution.py:557
  21.6 1.5 %collective-permute-start.5 = (bf16[4,2,64,128]{3,2,1,0:T(8,128)(2,1)S(1)}, bf16[4,2,64,128]{3,2,1,0:T(8,128)(2,1)S(1)}, u32[]{:S(2)}, u32[]{:S(2)}) collective-permute-start(bf16[4,2,64,128]{3,2,1,0:T(8,128)(2,1)S(1)} %pad_maximum_fusion.refs_2_.refs_6_), channel_id=1, source_target_pairs={{0,24},{8,0},{16,8},{24,16},{1,25},{9,1},{17,9},{25,17},{2,26},{10... | collective-permute-start | bytes 393224 | tf_op jit(solution)/shard_map/ppermute | solution.py:557
  23.0 1.5 %collective-permute-start.6 = (bf16[4,2,64,128]{3,2,1,0:T(8,128)(2,1)S(1)}, bf16[4,2,64,128]{3,2,1,0:T(8,128)(2,1)S(1)}, u32[]{:S(2)}, u32[]{:S(2)}) collective-permute-start(bf16[4,2,64,128]{3,2,1,0:T(8,128)(2,1)S(1)} %pad_maximum_fusion.refs_2_.refs_6_), channel_id=1, source_target_pairs={{0,16},{8,24},{16,0},{24,8},{1,17},{9,25},{17,1},{25,9},{2,18},{10... | collective-permute-start | bytes 393224 | tf_op jit(solution)/shard_map/ppermute | solution.py:557
  25.3 5.6 %diagonal.1 = (f32[2,8,1024]{2,1,0:T(8,128)}, f32[2,8,1024]{2,1,0:T(8,128)}, f32[2,128,1024]{2,1,0:T(8,128)}) custom-call(s32[4]{0:T(128)} %hits.1, s32[4,64]{1,0:T(4,128)} %refs_1_.11, bf16[4,2,64,128]{3,2,1,0:T(8,128)(2,1)} %copy-done.3, bf16[4,2,64,128]{3,2,1,0:T(8,128)(2,1)} %copy-done.18, bf16[1280,128]{1,0:T(8,128)(2,1)} %copy-done.9, ...), custom_call_target="tpu_custom_call" | custom-call | flops 2147483648 | bytes 2097152 | tf_op jit(solution)/shard_map/diagonal/pallas_call | solution.py:515
  30.9 1.0 collective-permute-start.3
  32.5 2.3 %collective-permute-start.9 = (bf16[16,2,64,128]{3,2,1,0:T(8,128)(2,1)S(1)}, bf16[16,2,64,128]{3,2,1,0:T(8,128)(2,1)S(1)}, u32[]{:S(2)}, u32[]{:S(2)}) collective-permute-start(bf16[16,2,64,128]{3,2,1,0:T(8,128)(2,1)S(1)} %all-to-all-done.refs_2_), channel_id=1, source_target_pairs={{0,24},{8,0},{16,8},{24,16},{1,25},{9,1},{17,9},{25,17},{2,26},{10... | collective-permute-start | bytes 1572872 | tf_op jit(solution)/shard_map/ppermute | solution.py:568
  35.6 0.8 copy-done.12
  36.4 18.0 %own.1 = (f32[2,8,1024]{2,1,0:T(8,128)}, f32[2,8,1024]{2,1,0:T(8,128)}, f32[2,128,1024]{2,1,0:T(8,128)}, bf16[2,64,128]{2,1,0:T(8,128)(2,1)}, bf16[2,64,128]{2,1...) custom-call(s32[4]{0:T(128)} %hits.1, s32[4,64]{1,0:T(4,128)} %refs_1_.11, ...), custom_call_target="tpu_custom_call" | custom-call | flops 15032385536 | bytes 2097152 | tf_op jit(solution)/shard_map/own/pallas_call | solution.py:515
  54.4 1.7 %collective-permute-start.14 = (bf16[2,64,128]{2,1,0:T(8,128)(2,1)}, bf16[2,64,128]{2,1,0:T(8,128)(2,1)S(1)}, u32[]{:S(2)}, u32[]{:S(2)}) collective-permute-start(bf16[2,64,128]{2,1,0:T(8,128)(2,1)} %get-tuple-element.83), channel_id=1, source_target_pairs={{0,2},{2,4},{4,6},{6,0},{1,3},{3,5},{5,7},{7,1},{8,10},{10,12},{12... | collective-permute-start | bytes 98312 | tf_op jit(solution)/shard_map/ppermute | solution.py:573
  56.2 2.4 %collective-permute-start.15 = (bf16[2,64,128]{2,1,0:T(8,128)(2,1)}, bf16[2,64,128]{2,1,0:T(8,128)(2,1)S(1)}, u32[]{:S(2)}, u32[]{:S(2)}) collective-permute-start(bf16[2,64,128]{2,1,0:T(8,128)(2,1)} %get-tuple-element.84), channel_id=1, source_target_pairs={{0,4},{2,6},{4,0},{6,2},{1,5},{3,7},{5,1},{7,3},{8,12},{10,14},{12... | collective-permute-start | bytes 98312 | tf_op jit(solution)/shard_map/ppermute | solution.py:573
  58.6 1.6 %collective-permute-start.10 = (bf16[16,2,64,128]{3,2,1,0:T(8,128)(2,1)S(1)}, bf16[16,2,64,128]{3,2,1,0:T(8,128)(2,1)S(1)}, u32[]{:S(2)}, u32[]{:S(2)}) collective-permute-start(bf16[16,2,64,128]{3,2,1,0:T(8,128)(2,1)S(1)} %collective-permute-done.8.refs_2_), channel_id=1, source_target_pairs={{0,1},{1,0},{2,3},{3,2},{4,5},{5,4},{6,7},{7,6},{8,9},{9,8},{10,11... | collective-permute-start | bytes 1572872 | tf_op jit(solution)/shard_map/ppermute | solution.py:536
  60.4 2.9 %collective-permute-start.12 = (bf16[8,2,64,128]{3,2,1,0:T(8,128)(2,1)S(1)}, bf16[8,2,64,128]{3,2,1,0:T(8,128)(2,1)S(1)}, u32[]{:S(2)}, u32[]{:S(2)}) collective-permute-start(bf16[8,2,64,128]{3,2,1,0:T(8,128)(2,1)S(1)} %slice.14), channel_id=1, source_target_pairs={{0,8},{8,16},{16,24},{24,0},{1,9},{9,17},{17,25},{25,1},{2,10},{10... | collective-permute-start | bytes 786440 | tf_op jit(solution)/shard_map/ppermute | solution.py:574
  63.2 8.0 %collective-permute-start.13 = (bf16[8,2,64,128]{3,2,1,0:T(8,128)(2,1)S(1)}, bf16[8,2,64,128]{3,2,1,0:T(8,128)(2,1)S(1)}, u32[]{:S(2)}, u32[]{:S(2)}) collective-permute-start(bf16[8,2,64,128]{3,2,1,0:T(8,128)(2,1)S(1)} %slice.15), channel_id=1, source_target_pairs={{0,24},{8,0},{16,8},{24,16},{1,25},{9,1},{17,9},{25,17},{2,26},{10... | collective-permute-start | bytes 786440 | tf_op jit(solution)/shard_map/ppermute | solution.py:575
  71.3 1.3 %collective-permute-start.16 = (bf16[2,64,128]{2,1,0:T(8,128)(2,1)S(1)}, bf16[2,64,128]{2,1,0:T(8,128)(2,1)S(1)}, u32[]{:S(2)}, u32[]{:S(2)}) collective-permute-start(bf16[2,64,128]{2,1,0:T(8,128)(2,1)S(1)} %copy-done.21), channel_id=1, source_target_pairs={{0,6},{2,0},{4,2},{6,4},{1,7},{3,1},{5,3},{7,5},{8,14},{10,8},{12,... | collective-permute-start | bytes 98312 | tf_op jit(solution)/shard_map/ppermute | solution.py:573
  72.5 8.7 %near.2 = (f32[2,8,1024]{2,1,0:T(8,128)}, f32[2,8,1024]{2,1,0:T(8,128)}, f32[2,128,1024]{2,1,0:T(8,128)}) custom-call(s32[4]{0:T(128)} %hits.1, s32[4,64]{1,0:T(4,128)} %refs_1_.11, bf16[16,2,64,128]{3,2,1,0:T(8,128)(2,1)} %copy-done.1, bf16[16,2,64,128]{3,2,1,0:T(8,128)(2,1)} %copy-done.2, bf16[1280,128]{1,0:T(8,128)(2,1)} %copy-done.9, ...), custom_call_target="tpu_custom_call" | custom-call | flops 8589934592 | bytes 2097152 | tf_op jit(solution)/shard_map/near/pallas_call | solution.py:515
  81.3 1.2 %collective-permute-start.17 = (bf16[8,2,64,128]{3,2,1,0:T(8,128)(2,1)S(1)}, bf16[8,2,64,128]{3,2,1,0:T(8,128)(2,1)S(1)}, u32[]{:S(2)}, u32[]{:S(2)}) collective-permute-start(bf16[8,2,64,128]{3,2,1,0:T(8,128)(2,1)S(1)} %collective-permute-done.12.refs_2_), channel_id=1, source_target_pairs={{0,1},{1,0},{2,3},{3,2},{4,5},{5,4},{6,7},{7,6},{8,9},{9,8},{10,11... | collective-permute-start | bytes 786440 | tf_op jit(solution)/shard_map/ppermute | solution.py:536
  83.5 0.8 copy-done.11
  84.3 8.8 %near.3 = (f32[2,8,1024]{2,1,0:T(8,128)}, f32[2,8,1024]{2,1,0:T(8,128)}, f32[2,128,1024]{2,1,0:T(8,128)}, bf16[2,64,512]{2,1,0:T(8,128)(2,1)}) custom-call(s32[4]{0:T(128)} %hits.1, s32[4,64]{1,0:T(4,128)} %refs_1_.11, bf16[16,2,64,128]{3,2,1,0:T(8,128)(2,1)} %copy-done.10, bf16[16,2,64,128]{3,2,1,0:T(8,128)(2,1)} %copy-done.11, ...), custom_call_target="tpu_custom_call" | custom-call | flops 8589934592 | bytes 2097152 | tf_op jit(solution)/shard_map/near/pallas_call | solution.py:515
  93.3 2.6 %collective-permute-start.22 = (bf16[2,64,512]{2,1,0:T(8,128)(2,1)}, bf16[2,64,512]{2,1,0:T(8,128)(2,1)S(1)}, u32[]{:S(2)}, u32[]{:S(2)}) collective-permute-start(bf16[2,64,512]{2,1,0:T(8,128)(2,1)} %get-tuple-element.110.refs_0_), channel_id=1, source_target_pairs={{0,96},{32,0},{64,32},{96,64},{1,97},{33,1},{65,33},{97,65},{2,98}... | collective-permute-start | bytes 393224 | tf_op jit(solution)/shard_map/ppermute | solution.py:583
  95.9 6.0 %far.2 = bf16[128,1024]{1,0:T(8,128)(2,1)} custom-call(s32[4]{0:T(128)} %hits.1, s32[4,64]{1,0:T(4,128)} %refs_1_.11, bf16[8,2,64,128]{3,2,1,0:T(8,128)(2,1)} %copy-done.14, bf16[8,2,64,128]{3,2,1,0:T(8,128)(2,1)} %copy-done.16, bf16[8,2,64,128]{3,2,1,0:T(8,128)(2,1)} %copy-done.15, bf16[8,2,64,128]{3,2,1,0:T(8,128)(2,1)} %copy-done.17, ...), custom_call_target="tpu_custom_call" | custom-call | flops 4294967296 | bytes 2097152 | tf_op jit(solution)/shard_map/far/pallas_call | solution.py:515
  102.0 3.3 %collective-permute-start.19 = (bf16[128,1024]{1,0:T(8,128)(2,1)}, bf16[128,1024]{1,0:T(8,128)(2,1)S(1)}, u32[]{:S(2)}, u32[]{:S(2)}) collective-permute-start(bf16[128,1024]{1,0:T(8,128)(2,1)} %far.2), channel_id=1, source_target_pairs={{0,0},{4,1},{2,2},{6,3},{1,4},{5,5},{3,6},{7,7},{8,8},{12,9},{10,1... | collective-permute-start | bytes 786440 | tf_op jit(solution)/shard_map/ppermute | solution.py:590
  105.4 5.8 %far.3 = bf16[128,1024]{1,0:T(8,128)(2,1)} custom-call(s32[4]{0:T(128)} %hits.1, s32[4,64]{1,0:T(4,128)} %refs_1_.11, bf16[8,2,64,128]{3,2,1,0:T(8,128)(2,1)} %copy-done.14, bf16[8,2,64,128]{3,2,1,0:T(8,128)(2,1)} %copy-done.16, bf16[8,2,64,128]{3,2,1,0:T(8,128)(2,1)} %copy-done.15, bf16[8,2,64,128]{3,2,1,0:T(8,128)(2,1)} %copy-done.17, ...), custom_call_target="tpu_custom_call" | custom-call | flops 4294967296 | bytes 2097152 | tf_op jit(solution)/shard_map/far/pallas_call | solution.py:515
  111.3 1.4 %collective-permute-start.23 = (bf16[128,1024]{1,0:T(8,128)(2,1)}, bf16[128,1024]{1,0:T(8,128)(2,1)S(1)}, u32[]{:S(2)}, u32[]{:S(2)}) collective-permute-start(bf16[128,1024]{1,0:T(8,128)(2,1)} %far.3), channel_id=1, source_target_pairs={{2,0},{6,1},{0,2},{4,3},{3,4},{7,5},{1,6},{5,7},{10,8},{14,9},{8,1... | collective-permute-start | bytes 786440 | tf_op jit(solution)/shard_map/ppermute | solution.py:590
  112.7 2.9 %place.1 = bf16[2,6,64,512]{3,2,1,0:T(8,128)(2,1)} custom-call(s32[4]{0:T(128)} %hits.1, s32[4,16]{1,0:T(4,128)} %dests.1, bf16[2,6,64,512]{3,2,1,0:T(8,128)(2,1)} %cache.3, bf16[2,64,512]{2,1,0:T(8,128)(2,1)} %get-tuple-element.110.refs_0_, bf16[2,64,512]{2,1,0:T(8,128)(2,1)} %copy-done.4, bf16[2,64,512]{2,1,0:T(8,128)(2,1)} %copy-done.5, ...), custom_call_target="tpu_custom_call" | custom-call | tf_op jit(solution)/shard_map/place/pallas_call | solution.py:160
  115.6 2.9 %collective-permute-done.23 = bf16[128,1024]{1,0:T(8,128)(2,1)S(1)} collective-permute-done((bf16[128,1024]{1,0:T(8,128)(2,1)}, bf16[128,1024]{1,0:T(8,128)(2,1)S(1)}, u32[]{:S(2)}, u32[]{:S(2)}) %collective-permute-start.23) | collective-permute-done | bytes 262176 | tf_op jit(solution)/shard_map/ppermute | solution.py:590
  118.6 0.9 maximum_select_fusion
  (82 shorter events, 3.3 us)
Async XLA Ops:
  2.8 14.4 %collective-permute-start.1 = (bf16[1280,128]{1,0:T(8,128)(2,1)}, bf16[1280,128]{1,0:T(8,128)(2,1)S(1)}, u32[]{:S(2)}, u32[]{:S(2)}) collective-permute-start(bf16[1280,128]{1,0:T(8,128)(2,1)} %get-tuple-element.58.after), channel_id=1, source_target_pairs={{0,2},{1,6},{2,0},{3,4},{4,3},{5,7},{6,1},{7,5},{8,10},{9,14},{10,... | collective-permute-start | bytes 983048 | tf_op jit(solution)/shard_map/ppermute | solution.py:553
  7.0 10.2 %collective-permute-start = (bf16[1280,128]{1,0:T(8,128)(2,1)}, bf16[1280,128]{1,0:T(8,128)(2,1)S(1)}, u32[]{:S(2)}, u32[]{:S(2)}) collective-permute-start(bf16[1280,128]{1,0:T(8,128)(2,1)} %get-tuple-element.59), channel_id=1, source_target_pairs={{0,0},{1,4},{2,2},{3,6},{4,1},{5,5},{6,3},{7,7},{8,8},{9,12},{10,1... | collective-permute-start | bytes 983048 | tf_op jit(solution)/shard_map/ppermute | solution.py:552
  11.9 19.0 %all-to-all-start = ((bf16[16,2,64,128]{3,2,1,0:T(8,128)(2,1)}), bf16[16,2,64,128]{3,2,1,0:T(8,128)(2,1)S(1)}, u32[]{:S(2)}, u32[]{:S(2)}) async-start(bf16[16,2,64,128]{3,2,1,0:T(8,128)(2,1)} %pack.1), calls=%async_computation | async-start | bytes 1048576 | tf_op jit(solution)/shard_map/all_to_all | solution.py:564
  17.1 7.4 %copy-start.8 = (bf16[1280,128]{1,0:T(8,128)(2,1)}, bf16[1280,128]{1,0:T(8,128)(2,1)S(1)}, u32[]{:S(2)}) copy-start(bf16[1280,128]{1,0:T(8,128)(2,1)S(1)} %collective-permute-done.1.refs_5_.refs_9_.refs_7_) | copy-start | bytes 983044
  17.2 7.4 %copy-start.9 = (bf16[1280,128]{1,0:T(8,128)(2,1)}, bf16[1280,128]{1,0:T(8,128)(2,1)S(1)}, u32[]{:S(2)}) copy-start(bf16[1280,128]{1,0:T(8,128)(2,1)S(1)} %collective-permute-done.refs_4_.refs_8_.refs_6_) | copy-start | bytes 983044
  17.2 7.4 %collective-permute-start.2 = (bf16[4,2,64,128]{3,2,1,0:T(8,128)(2,1)S(1)}, bf16[4,2,64,128]{3,2,1,0:T(8,128)(2,1)S(1)}, u32[]{:S(2)}, u32[]{:S(2)}) collective-permute-start(bf16[4,2,64,128]{3,2,1,0:T(8,128)(2,1)S(1)} %pad_maximum_fusion.refs_2_.refs_6_), channel_id=1, source_target_pairs={{0,1},{1,0},{2,3},{3,2},{4,5},{5,4},{6,7},{7,6},{8,9},{9,8},{10,11... | collective-permute-start | bytes 393224 | tf_op jit(solution)/shard_map/ppermute | solution.py:536
  20.4 10.5 %collective-permute-start.4 = (bf16[4,2,64,128]{3,2,1,0:T(8,128)(2,1)S(1)}, bf16[4,2,64,128]{3,2,1,0:T(8,128)(2,1)S(1)}, u32[]{:S(2)}, u32[]{:S(2)}) collective-permute-start(bf16[4,2,64,128]{3,2,1,0:T(8,128)(2,1)S(1)} %pad_maximum_fusion.refs_2_.refs_6_), channel_id=1, source_target_pairs={{0,8},{8,16},{16,24},{24,0},{1,9},{9,17},{17,25},{25,1},{2,10},{10... | collective-permute-start | bytes 393224 | tf_op jit(solution)/shard_map/ppermute | solution.py:557
  21.6 10.3 %collective-permute-start.5 = (bf16[4,2,64,128]{3,2,1,0:T(8,128)(2,1)S(1)}, bf16[4,2,64,128]{3,2,1,0:T(8,128)(2,1)S(1)}, u32[]{:S(2)}, u32[]{:S(2)}) collective-permute-start(bf16[4,2,64,128]{3,2,1,0:T(8,128)(2,1)S(1)} %pad_maximum_fusion.refs_2_.refs_6_), channel_id=1, source_target_pairs={{0,24},{8,0},{16,8},{24,16},{1,25},{9,1},{17,9},{25,17},{2,26},{10... | collective-permute-start | bytes 393224 | tf_op jit(solution)/shard_map/ppermute | solution.py:557
  23.0 8.9 %collective-permute-start.6 = (bf16[4,2,64,128]{3,2,1,0:T(8,128)(2,1)S(1)}, bf16[4,2,64,128]{3,2,1,0:T(8,128)(2,1)S(1)}, u32[]{:S(2)}, u32[]{:S(2)}) collective-permute-start(bf16[4,2,64,128]{3,2,1,0:T(8,128)(2,1)S(1)} %pad_maximum_fusion.refs_2_.refs_6_), channel_id=1, source_target_pairs={{0,16},{8,24},{16,0},{24,8},{1,17},{9,25},{17,1},{25,9},{2,18},{10... | collective-permute-start | bytes 393224 | tf_op jit(solution)/shard_map/ppermute | solution.py:557
  30.9 3.9 %collective-permute-start.3 = (bf16[16,2,64,128]{3,2,1,0:T(8,128)(2,1)S(1)}, bf16[16,2,64,128]{3,2,1,0:T(8,128)(2,1)S(1)}, u32[]{:S(2)}, u32[]{:S(2)}) collective-permute-start(bf16[16,2,64,128]{3,2,1,0:T(8,128)(2,1)S(1)} %all-to-all-done.refs_2_), channel_id=1, source_target_pairs={{0,1},{1,0},{2,3},{3,2},{4,5},{5,4},{6,7},{7,6},{8,9},{9,8},{10,11... | collective-permute-start | bytes 1572872 | tf_op jit(solution)/shard_map/ppermute | solution.py:536
  32.0 2.8 %collective-permute-start.7 = (bf16[12,2,64,128]{3,2,1,0:T(8,128)(2,1)S(1)}, bf16[12,2,64,128]{3,2,1,0:T(8,128)(2,1)S(1)}, u32[]{:S(2)}, u32[]{:S(2)}) collective-permute-start(bf16[12,2,64,128]{3,2,1,0:T(8,128)(2,1)S(1)} %constant_dynamic-update-slice_fusion.refs_4_), channel_id=1, source_target_pairs={{0,1},{1,0},{2,3},{3,2},{4,5},{5,4},{6,7},{7,6},{8,9},{9,8},{10,11... | collective-permute-start | bytes 1179656 | tf_op jit(solution)/shard_map/ppermute | solution.py:536
  32.1 22.3 %collective-permute-start.8 = (bf16[16,2,64,128]{3,2,1,0:T(8,128)(2,1)S(1)}, bf16[16,2,64,128]{3,2,1,0:T(8,128)(2,1)S(1)}, u32[]{:S(2)}, u32[]{:S(2)}) collective-permute-start(bf16[16,2,64,128]{3,2,1,0:T(8,128)(2,1)S(1)} %all-to-all-done.refs_2_), channel_id=1, source_target_pairs={{0,8},{8,16},{16,24},{24,0},{1,9},{9,17},{17,25},{25,1},{2,10},{10... | collective-permute-start | bytes 1572872 | tf_op jit(solution)/shard_map/ppermute | solution.py:567
  32.5 22.0 %collective-permute-start.9 = (bf16[16,2,64,128]{3,2,1,0:T(8,128)(2,1)S(1)}, bf16[16,2,64,128]{3,2,1,0:T(8,128)(2,1)S(1)}, u32[]{:S(2)}, u32[]{:S(2)}) collective-permute-start(bf16[16,2,64,128]{3,2,1,0:T(8,128)(2,1)S(1)} %all-to-all-done.refs_2_), channel_id=1, source_target_pairs={{0,24},{8,0},{16,8},{24,16},{1,25},{9,1},{17,9},{25,17},{2,26},{10... | collective-permute-start | bytes 1572872 | tf_op jit(solution)/shard_map/ppermute | solution.py:568
  54.4 8.8 %collective-permute-start.14 = (bf16[2,64,128]{2,1,0:T(8,128)(2,1)}, bf16[2,64,128]{2,1,0:T(8,128)(2,1)S(1)}, u32[]{:S(2)}, u32[]{:S(2)}) collective-permute-start(bf16[2,64,128]{2,1,0:T(8,128)(2,1)} %get-tuple-element.83), channel_id=1, source_target_pairs={{0,2},{2,4},{4,6},{6,0},{1,3},{3,5},{5,7},{7,1},{8,10},{10,12},{12... | collective-permute-start | bytes 98312 | tf_op jit(solution)/shard_map/ppermute | solution.py:573
  56.2 15.1 %collective-permute-start.15 = (bf16[2,64,128]{2,1,0:T(8,128)(2,1)}, bf16[2,64,128]{2,1,0:T(8,128)(2,1)S(1)}, u32[]{:S(2)}, u32[]{:S(2)}) collective-permute-start(bf16[2,64,128]{2,1,0:T(8,128)(2,1)} %get-tuple-element.84), channel_id=1, source_target_pairs={{0,4},{2,6},{4,0},{6,2},{1,5},{3,7},{5,1},{7,3},{8,12},{10,14},{12... | collective-permute-start | bytes 98312 | tf_op jit(solution)/shard_map/ppermute | solution.py:573
  58.6 12.7 %copy-start.21 = (bf16[2,64,128]{2,1,0:T(8,128)(2,1)S(1)}, bf16[2,64,128]{2,1,0:T(8,128)(2,1)}, u32[]{:S(2)}) copy-start(bf16[2,64,128]{2,1,0:T(8,128)(2,1)} %get-tuple-element.85) | copy-start | bytes 98308
  58.6 24.1 %collective-permute-start.10 = (bf16[16,2,64,128]{3,2,1,0:T(8,128)(2,1)S(1)}, bf16[16,2,64,128]{3,2,1,0:T(8,128)(2,1)S(1)}, u32[]{:S(2)}, u32[]{:S(2)}) collective-permute-start(bf16[16,2,64,128]{3,2,1,0:T(8,128)(2,1)S(1)} %collective-permute-done.8.refs_2_), channel_id=1, source_target_pairs={{0,1},{1,0},{2,3},{3,2},{4,5},{5,4},{6,7},{7,6},{8,9},{9,8},{10,11... | collective-permute-start | bytes 1572872 | tf_op jit(solution)/shard_map/ppermute | solution.py:536
  60.3 22.4 %collective-permute-start.11 = (bf16[16,2,64,128]{3,2,1,0:T(8,128)(2,1)S(1)}, bf16[16,2,64,128]{3,2,1,0:T(8,128)(2,1)S(1)}, u32[]{:S(2)}, u32[]{:S(2)}) collective-permute-start(bf16[16,2,64,128]{3,2,1,0:T(8,128)(2,1)S(1)} %collective-permute-done.9.refs_3_), channel_id=1, source_target_pairs={{0,1},{1,0},{2,3},{3,2},{4,5},{5,4},{6,7},{7,6},{8,9},{9,8},{10,11... | collective-permute-start | bytes 1572872 | tf_op jit(solution)/shard_map/ppermute | solution.py:536
  60.4 20.9 %collective-permute-start.12 = (bf16[8,2,64,128]{3,2,1,0:T(8,128)(2,1)S(1)}, bf16[8,2,64,128]{3,2,1,0:T(8,128)(2,1)S(1)}, u32[]{:S(2)}, u32[]{:S(2)}) collective-permute-start(bf16[8,2,64,128]{3,2,1,0:T(8,128)(2,1)S(1)} %slice.14), channel_id=1, source_target_pairs={{0,8},{8,16},{16,24},{24,0},{1,9},{9,17},{17,25},{25,1},{2,10},{10... | collective-permute-start | bytes 786440 | tf_op jit(solution)/shard_map/ppermute | solution.py:574
  63.2 18.0 %copy-start.19 = (bf16[2,64,128]{2,1,0:T(8,128)(2,1)}, bf16[2,64,128]{2,1,0:T(8,128)(2,1)S(1)}, u32[]{:S(2)}) copy-start(bf16[2,64,128]{2,1,0:T(8,128)(2,1)S(1)} %collective-permute-done.14.refs_5_) | copy-start | bytes 98308
  63.2 18.1 %collective-permute-start.13 = (bf16[8,2,64,128]{3,2,1,0:T(8,128)(2,1)S(1)}, bf16[8,2,64,128]{3,2,1,0:T(8,128)(2,1)S(1)}, u32[]{:S(2)}, u32[]{:S(2)}) collective-permute-start(bf16[8,2,64,128]{3,2,1,0:T(8,128)(2,1)S(1)} %slice.15), channel_id=1, source_target_pairs={{0,24},{8,0},{16,8},{24,16},{1,25},{9,1},{17,9},{25,17},{2,26},{10... | collective-permute-start | bytes 786440 | tf_op jit(solution)/shard_map/ppermute | solution.py:575
  71.3 10.0 %copy-start.20 = (bf16[2,64,128]{2,1,0:T(8,128)(2,1)}, bf16[2,64,128]{2,1,0:T(8,128)(2,1)S(1)}, u32[]{:S(2)}) copy-start(bf16[2,64,128]{2,1,0:T(8,128)(2,1)S(1)} %collective-permute-done.15.refs_6_) | copy-start | bytes 98308
  71.3 10.0 %collective-permute-start.16 = (bf16[2,64,128]{2,1,0:T(8,128)(2,1)S(1)}, bf16[2,64,128]{2,1,0:T(8,128)(2,1)S(1)}, u32[]{:S(2)}, u32[]{:S(2)}) collective-permute-start(bf16[2,64,128]{2,1,0:T(8,128)(2,1)S(1)} %copy-done.21), channel_id=1, source_target_pairs={{0,6},{2,0},{4,2},{6,4},{1,7},{3,1},{5,3},{7,5},{8,14},{10,8},{12,... | collective-permute-start | bytes 98312 | tf_op jit(solution)/shard_map/ppermute | solution.py:573
  81.3 11.8 %copy-start.14 = (bf16[8,2,64,128]{3,2,1,0:T(8,128)(2,1)}, bf16[8,2,64,128]{3,2,1,0:T(8,128)(2,1)S(1)}, u32[]{:S(2)}) copy-start(bf16[8,2,64,128]{3,2,1,0:T(8,128)(2,1)S(1)} %collective-permute-done.12.refs_2_) | copy-start | bytes 786436
  81.3 11.8 %copy-start.15 = (bf16[8,2,64,128]{3,2,1,0:T(8,128)(2,1)}, bf16[8,2,64,128]{3,2,1,0:T(8,128)(2,1)S(1)}, u32[]{:S(2)}) copy-start(bf16[8,2,64,128]{3,2,1,0:T(8,128)(2,1)S(1)} %collective-permute-done.13.refs_4_) | copy-start | bytes 786436
  81.3 11.8 %collective-permute-start.17 = (bf16[8,2,64,128]{3,2,1,0:T(8,128)(2,1)S(1)}, bf16[8,2,64,128]{3,2,1,0:T(8,128)(2,1)S(1)}, u32[]{:S(2)}, u32[]{:S(2)}) collective-permute-start(bf16[8,2,64,128]{3,2,1,0:T(8,128)(2,1)S(1)} %collective-permute-done.12.refs_2_), channel_id=1, source_target_pairs={{0,1},{1,0},{2,3},{3,2},{4,5},{5,4},{6,7},{7,6},{8,9},{9,8},{10,11... | collective-permute-start | bytes 786440 | tf_op jit(solution)/shard_map/ppermute | solution.py:536
  82.6 10.6 %collective-permute-start.18 = (bf16[8,2,64,128]{3,2,1,0:T(8,128)(2,1)S(1)}, bf16[8,2,64,128]{3,2,1,0:T(8,128)(2,1)S(1)}, u32[]{:S(2)}, u32[]{:S(2)}) collective-permute-start(bf16[8,2,64,128]{3,2,1,0:T(8,128)(2,1)S(1)} %collective-permute-done.13.refs_4_), channel_id=1, source_target_pairs={{0,1},{1,0},{2,3},{3,2},{4,5},{5,4},{6,7},{7,6},{8,9},{9,8},{10,11... | collective-permute-start | bytes 786440 | tf_op jit(solution)/shard_map/ppermute | solution.py:536
  93.2 12.2 %collective-permute-start.20 = (bf16[2,64,512]{2,1,0:T(8,128)(2,1)}, bf16[2,64,512]{2,1,0:T(8,128)(2,1)S(1)}, u32[]{:S(2)}, u32[]{:S(2)}) collective-permute-start(bf16[2,64,512]{2,1,0:T(8,128)(2,1)} %get-tuple-element.110.refs_0_), channel_id=1, source_target_pairs={{0,32},{32,64},{64,96},{96,0},{1,33},{33,65},{65,97},{97,1},{2,34}... | collective-permute-start | bytes 393224 | tf_op jit(solution)/shard_map/ppermute | solution.py:583
  93.3 12.1 %collective-permute-start.21 = (bf16[2,64,512]{2,1,0:T(8,128)(2,1)}, bf16[2,64,512]{2,1,0:T(8,128)(2,1)S(1)}, u32[]{:S(2)}, u32[]{:S(2)}) collective-permute-start(bf16[2,64,512]{2,1,0:T(8,128)(2,1)} %get-tuple-element.110.refs_0_), channel_id=1, source_target_pairs={{0,64},{32,96},{64,0},{96,32},{1,65},{33,97},{65,1},{97,33},{2,66}... | collective-permute-start | bytes 393224 | tf_op jit(solution)/shard_map/ppermute | solution.py:583
  93.3 12.0 %collective-permute-start.22 = (bf16[2,64,512]{2,1,0:T(8,128)(2,1)}, bf16[2,64,512]{2,1,0:T(8,128)(2,1)S(1)}, u32[]{:S(2)}, u32[]{:S(2)}) collective-permute-start(bf16[2,64,512]{2,1,0:T(8,128)(2,1)} %get-tuple-element.110.refs_0_), channel_id=1, source_target_pairs={{0,96},{32,0},{64,32},{96,64},{1,97},{33,1},{65,33},{97,65},{2,98}... | collective-permute-start | bytes 393224 | tf_op jit(solution)/shard_map/ppermute | solution.py:583
  102.0 13.6 %collective-permute-start.19 = (bf16[128,1024]{1,0:T(8,128)(2,1)}, bf16[128,1024]{1,0:T(8,128)(2,1)S(1)}, u32[]{:S(2)}, u32[]{:S(2)}) collective-permute-start(bf16[128,1024]{1,0:T(8,128)(2,1)} %far.2), channel_id=1, source_target_pairs={{0,0},{4,1},{2,2},{6,3},{1,4},{5,5},{3,6},{7,7},{8,8},{12,9},{10,1... | collective-permute-start | bytes 786440 | tf_op jit(solution)/shard_map/ppermute | solution.py:590
  111.3 7.3 %collective-permute-start.23 = (bf16[128,1024]{1,0:T(8,128)(2,1)}, bf16[128,1024]{1,0:T(8,128)(2,1)S(1)}, u32[]{:S(2)}, u32[]{:S(2)}) collective-permute-start(bf16[128,1024]{1,0:T(8,128)(2,1)} %far.3), channel_id=1, source_target_pairs={{2,0},{6,1},{0,2},{4,3},{3,4},{7,5},{1,6},{5,7},{10,8},{14,9},{8,1... | collective-permute-start | bytes 786440 | tf_op jit(solution)/shard_map/ppermute | solution.py:590
  (16 other events, 54.2 us)
where the time goes:
time: 119 us
  Pallas kernels  60.9 us (51%)
  starting transfers between devices  49.6 us (42%)
  local copies, waits for them, and re-layouts  3.92 us (3%)
  waiting for transfers between devices  3 us (3%)
    pallas_call x6, Pallas kernels, attend(): pl.pallas_call(functools.partial(attend_kernel, plan, len(sources), chose...  53 us
    ppermute x1, starting transfers between devices, shards(): far_b = lax.ppermute(right[HALF:], 'x', shift(4, -1))  8.04 us
    ppermute x7, starting transfers between devices, swap(): return lax.ppermute(part, 'c', shift(2, 1))  7.27 us
    ppermute x3, starting transfers between devices, shards(): lax.ppermute(parts[k], 'y', shift(4, k))  5.36 us
    all_to_all x1, starting transfers between devices, shards(): own = lax.all_to_all(sent, ('s', 'y'), 0, 0, tiled=True)  5.26 us
    ppermute x2, starting transfers between devices, shards(): outs.append(lax.ppermute(out, yc, back))  4.75 us
    ppermute x3, starting transfers between devices, shards(): rest = [lax.ppermute(fresh, 'x', shift(4, -k)) for k in NEIGHBOURS]  4.22 us
    ppermute x1, starting transfers between devices, shards(): msg_b = lax.ppermute(msg_b, yc, to_b)  4.2 us
  transfers between devices with their start and end apart: 25, of which 1 were waited for; matrix products, arithmetic and copies ran while one was open for 0% of the time, Pallas kernels for 49%

commit v1 on v0

--- a/solution.py
+++ b/solution.py
@@ -14,7 +14,6 @@
 SMALL = 8
 ROWS = 1024
 MESSAGE = ROWS + 4 * SUB
-HALF = 8
 NEG_FILL = -1e30
 LOG2E = float(np.log2(np.e))
 SCALE = HD ** (-0.5) * LOG2E
@@ -28,8 +27,8 @@
 F32 = jnp.float32
 
 
-def params():
-    return pltpu.CompilerParams(vmem_limit_bytes=60 << 20)
+def params(mib=60):
+    return pltpu.CompilerParams(vmem_limit_bytes=mib << 20)
 
 
 def position():
@@ -149,7 +148,10 @@
     for i in range(slots):
         copies.start(cache.at[:, i], held.at[:, i], when=slot != i)
     for k in range(4):
-        copies.start(arrived[k], held.at[:, slot], when=away == k)
+        for piece in range(4):
+            cols = pl.ds(pl.multiple_of((my_y - piece + 4) % 4 * HD, HD), HD)
+            part = arrived[k].at[pl.ds(2 * piece, 2)]
+            copies.start(part, held.at[:, slot, :, cols], when=away == k)
     copies.wait()
     copies = Copies(sems)
     copies.start(held, out)
@@ -162,7 +164,7 @@
         out_shape=jax.ShapeDtypeStruct(cache.shape, cache.dtype),
         in_specs=[SMEM, SMEM, ANY] + [ANY] * 4,
         out_specs=ANY,
-        scratch_shapes=[pltpu.VMEM(cache.shape, BF16), pltpu.SemaphoreType.DMA((10,))],
+        scratch_shapes=[pltpu.VMEM(cache.shape, BF16), pltpu.SemaphoreType.DMA((22,))],
         compiler_params=params(),
         name="place",
     )(hits, dests, cache, *arrived)
@@ -194,6 +196,11 @@
     fold_values(weights.astype(BF16), values, 1.0, l, acc)
 
 
+def both_of(kv, begin, size):
+    part = kv.at[pl.ds(begin, size)]
+    return part[:, 0].reshape(size * SUB, HD), part[:, 1].reshape(size * SUB, HD)
+
+
 def state_shapes(rows):
     return [(rows, 8, ROWS), (rows, 8, ROWS), (rows, HD, ROWS)]
 
@@ -203,40 +210,42 @@
     return pl.CostEstimate(flops=16 * HD * units, bytes_accessed=1 << 21, transcendentals=units)
 
 
-def keys_at(offset, sources):
+def side(mine):
+    return jnp.where((position()[3] == 0) == mine, 3, 1)
+
+
+def keys_at(offset, pieces):
     def start(hits, table, refs, fetch, slot):
         my_store, my_x, _, _ = position()
-        other_x = (my_x + offset) % 4
+        other_x = (my_x + offset()) % 4
         hit_count = hits[my_store]
-        step = min(len(sources), 2)
-
-        def both(index, slot):
-            if len(sources) <= 2:
-                for k, source in enumerate(sources):
-                    fetch(refs[source], index, slot + k).start(priority=1)
-                return
-            for low, pair in ((True, sources[:2]), (False, sources[2:])):
-                at = index if low else index - HALF
-
-                @pl.when((index < HALF) if low else (index >= HALF))
-                def _(at=at, pair=pair):
-                    fetch(refs[pair[0]], at, slot).start(priority=1)
-                    fetch(refs[pair[1]], at, slot + 1).start(priority=1)
-
-        for turn in range(4):
-
-            def one(near, slot, turn=turn):
-                block = other_x * 4 + near + 16 * turn
-                used = block < hit_count
-
-                @pl.when(used)
-                def _():
-                    both(table[my_store, block] // 96 * 4 + near, slot)
-
-                return jnp.where(used, slot + step, slot)
-
-            slot = lax.fori_loop(0, 4, one, slot)
-        return slot
+        whole = hit_count >= 64
+
+        @pl.when(whole)
+        def _():
+            for k, (source, base) in enumerate(pieces):
+                for part in (0, 8):
+                    fetch(refs[source], base + part, slot + 16 * k + part, 8).start(priority=1)
+
+        def turns(slot):
+            for turn in range(4):
+
+                def one(near, slot, turn=turn):
+                    block = other_x * 4 + near + 16 * turn
+                    used = block < hit_count
+
+                    @pl.when(used)
+                    def _():
+                        index = table[my_store, block] // 96 * 4 + near
+                        for k, (source, base) in enumerate(pieces):
+                            fetch(refs[source], base + index, slot + k, 1).start(priority=1)
+
+                    return jnp.where(used, slot + 2, slot)
+
+                slot = lax.fori_loop(0, 4, one, slot)
+            return slot
+
+        return lax.cond(whole, lambda at: at + 32, turns, slot)
 
     return start
 
@@ -244,18 +253,16 @@
 NEIGHBOURS = (3, 1, 2)
 
 
-def earlier_rows(sources):
-    def start(hits, table, refs, fetch, slot):
+def earlier_rows(mine, other):
+    def start(refs, fetch, slot):
         _, my_x, _, _ = position()
         for place, offset in enumerate(NEIGHBOURS):
             earlier = (my_x + offset) % 4 < my_x
 
             @pl.when(earlier)
             def _(place=place, slot=slot):
-                for k, source in enumerate(sources):
-                    for part in range(4):
-                        at = slot + 4 * k + part
-                        fetch(refs[source], 4 * place + part, at).start(priority=1)
+                fetch(refs[mine], 4 * place, slot, 4).start(priority=1)
+                fetch(refs[other], 4 * place, slot + 4, 4, slot).start(priority=1)
 
             slot = jnp.where(earlier, slot + 8, slot)
         return slot
@@ -265,25 +272,29 @@
 
 def route(hits, sources, held, sems):
     my_store, my_x, my_y, my_core = position()
-    own, own_other, rest, rest_other = sources
     for k in range(4):
         near = (my_y + k) % 4
         block = (my_x * 4 + near - hits[my_store] + 64) % 16
         spot = block % 4
         away = (block // 4 - my_x + 4) % 4
+        same = spot // 2 == my_core
         index = 2 * ((spot + my_y) % 2) + my_core
-        place = jnp.where(away == 3, 0, away)
-        for here in (True, False):
-            for same in (True, False):
-                source = (own if same else own_other) if here else (rest if same else rest_other)
-                at = index if here else 4 * place + index
-
-                @pl.when(((away == 0) == here) & ((spot // 2 == my_core) == same))
-                def _(source=source, at=at, k=k):
-                    pltpu.make_async_copy(source.at[at], held.at[k], sems.at[k]).start(priority=1)
-
-
-def attend_kernel(plan, n_sources, chosen, first, last, extra, *refs):
+        far = 4 * jnp.where(away == 3, 0, away) + index
+        places = (
+            (away == 0) & same,
+            (away == 0) & jnp.logical_not(same),
+            (away != 0) & same,
+            (away != 0) & jnp.logical_not(same),
+        )
+        for which, (source, here) in enumerate(zip(sources, places)):
+            at = index if which < 2 else far
+
+            @pl.when(here)
+            def _(source=source, at=at, k=k):
+                pltpu.make_async_copy(source.at[at], held.at[k], sems.at[k]).start(priority=1)
+
+
+def attend_kernel(plan, early, n_sources, chosen, first, last, extra, *refs):
     hits, table = refs[:2]
     sources = refs[2 : 2 + n_sources]
     refs = refs[2 + n_sources :]
@@ -296,11 +307,8 @@
         spare = refs[-2:]
         refs = refs[:-2]
     if extra == "route":
-        moved, sources = sources[-4:], sources[:-2]
+        moved = sources[-4:]
         n_moved = 4
-    elif extra == "join":
-        moved, sources = sources[-4:], sources[:-4]
-        n_moved = 1
     else:
         n_moved = 0
     n_outs = rows if last else 3
@@ -312,10 +320,10 @@
     state = (m, l, acc)
     _, _, my_y, my_core = position()
 
-    def fetch(source, index, slot):
-        start = pl.multiple_of(slot * SUB, SUB)
+    def fetch(source, index, slot, size, signal=None):
+        signal = slot if signal is None else signal
         return pltpu.make_async_copy(
-            source.at[index], kv.at[:, pl.ds(start, SUB), :], sems.at[slot]
+            source.at[pl.ds(index, size)], kv.at[pl.ds(slot, size)], sems.at[signal]
         )
 
     held, held_sems = spare if extra else (None, None)
@@ -328,17 +336,19 @@
             owner = my_core if which == 0 else 1 - my_core
             for block in range(2):
                 spot = 2 * owner + (my_y + block) % 2
-                for half in range(2):
-                    at = pl.ds(pl.multiple_of((2 * spot + half) * SUB, SUB), SUB)
-                    loads.start(source.at[2 * block + half], near.at[:, at, :])
+                loads.start(source.at[pl.ds(2 * block, 2)], near.at[pl.ds(2 * spot, 2)])
     else:
         l_old, acc_old = refs[:2]
         for i, r in enumerate(chosen):
             loads.start(state_in[0].at[r], m.at[i])
 
-    count = jnp.int32(0)
-    for start in plan:
-        count = start(hits, table, sources, fetch, count)
+    new = jnp.int32(0)
+    if early is not None:
+        new = early(sources, fetch, new)
+    count = new
+    if plan is not None:
+        count = plan(hits, table, sources, fetch, count)
+    whole = hits[lax.axis_index("s")] >= 64
 
     later = Copies(more.at[pl.ds(len(loads.all), 2 * rows)])
     if not first:
@@ -347,32 +357,45 @@
             later.start(state_in[2].at[r], acc_old.at[i])
 
     if extra == "route":
-        route(hits, (moved[2], moved[3], moved[0], moved[1]), held, held_sems)
-    if extra == "join":
-        for k in range(4):
-            cols = pl.ds(pl.multiple_of((my_y - k + 4) % 4 * HD, HD), HD)
-            pltpu.make_async_copy(moved[k], held.at[:, :, cols], held_sems.at[k]).start(priority=1)
-
+        route(hits, moved, held, held_sems)
     def diagonal(i):
         shape = (8 * SUB, ROWS)
         spot = 2 * my_core + (my_y + i + chosen[0]) % 2
         key_at = lax.broadcasted_iota(jnp.int32, shape, 0)
         row_at = lax.broadcasted_iota(jnp.int32, shape, 1) % HD + spot * HD
         allowed = key_at <= row_at
-        exact_fold(q[i], near[0], near[1], allowed, m.at[i], l.at[i], acc.at[i])
+        keys, values = both_of(near, 0, 8)
+        exact_fold(q[i], keys, values, allowed, m.at[i], l.at[i], acc.at[i])
 
     def clear_state(i):
         l[i] = jnp.zeros(l.shape[1:], F32)
         acc[i] = jnp.zeros(acc.shape[1:], F32)
 
-    def wait(slot, _):
-        fetch(sources[0], 0, slot).wait()
-        return 0
+    def wait(begin, end):
+        def some(group, _):
+            slot = begin + 8 * group
+            by_eight = whole | (slot < new)
+
+            @pl.when(by_eight)
+            def _():
+                pltpu.make_async_copy(
+                    kv.at[pl.ds(0, 8)], kv.at[pl.ds(slot, 8)], sems.at[slot]
+                ).wait()
+
+            @pl.when(jnp.logical_not(by_eight))
+            def _():
+                def one(at, _):
+                    pltpu.make_async_copy(kv.at[0], kv.at[at], sems.at[at]).wait()
+                    return 0
+
+                lax.fori_loop(slot, jnp.minimum(slot + 8, end), one, 0)
+
+            return 0
+
+        lax.fori_loop(0, (end - begin + 7) // 8, some, 0)
 
     def tile(i, fold, begin, size, masked):
-        start = pl.multiple_of(begin * SUB, SUB)
-        keys = kv[0, pl.ds(start, size * SUB), :]
-        values = kv[1, pl.ds(start, size * SUB), :]
+        keys, values = both_of(kv, begin, size)
         allowed = None
         if masked:
             at = lax.broadcasted_iota(jnp.int32, (size * SUB, ROWS), 0)
@@ -396,7 +419,7 @@
         def arrive(begin, end):
             @pl.when(i == 0)
             def _():
-                lax.fori_loop(begin, end, wait, 0)
+                wait(begin, end)
 
         def full(t, _):
             arrive(t * TILE, (t + 1) * TILE)
@@ -415,8 +438,7 @@
             arrive(rest, count)
 
             def clear(slot, _):
-                start = pl.multiple_of(slot * SUB, SUB)
-                kv[:, pl.ds(start, SUB), :] = jnp.zeros((2, SUB, HD), BF16)
+                kv[slot] = jnp.zeros((2, SUB, HD), BF16)
                 return 0
 
             lax.fori_loop(count, rest + SMALL, clear, 0)
@@ -463,13 +485,6 @@
         for k in range(4):
             sent.start(held.at[k], moved_outs[k])
         sent.wait()
-    if extra == "join":
-        for k in range(4):
-            cols = pl.ds(0, HD)
-            pltpu.make_async_copy(moved[k], held.at[:, :, cols], held_sems.at[k]).wait()
-        sent = Copies(held_sems)
-        sent.start(held, moved_outs[0])
-        sent.wait()
     for i in range(rows):
         if last:
             copy = pltpu.make_async_copy(refs[2].at[i], outs[i], stored.at[i])
@@ -480,7 +495,7 @@
                 pltpu.make_async_copy(here.at[i], there.at[i], stored.at[3 * i + k]).wait()
 
 
-def attend(hits, table, plan, most, sources, messages, state, chosen, name, extra=None):
+def attend(hits, table, plan, early, most, sources, messages, state, chosen, name, extra=None):
     first = not state
     last = name == "far"
     rows = len(chosen)
@@ -493,13 +508,13 @@
     scratch = [pltpu.VMEM(s, F32) for s in shapes]
     scratch += [
         pltpu.VMEM((rows, ROWS, HD), BF16),
-        pltpu.VMEM((2, room * SUB, HD), BF16),
+        pltpu.VMEM((room, 2, SUB, HD), BF16),
         pltpu.SemaphoreType.DMA((room,)),
-        pltpu.SemaphoreType.DMA(((8 if first else rows) + 3 * rows,)),
+        pltpu.SemaphoreType.DMA(((6 if first else rows) + 3 * rows,)),
         pltpu.SemaphoreType.DMA((3 * rows,)),
     ]
     if first:
-        scratch.append(pltpu.VMEM((2, 8 * SUB, HD), BF16))
+        scratch.append(pltpu.VMEM((8, 2, SUB, HD), BF16))
     else:
         scratch += [pltpu.VMEM(s, F32) for s in shapes[1:]]
     if last:
@@ -507,19 +522,16 @@
     if extra == "route":
         out_shape += [jax.ShapeDtypeStruct((2, SUB, HD), BF16)] * 4
         scratch.append(pltpu.VMEM((4, 2, SUB, HD), BF16))
-    if extra == "join":
-        out_shape += [jax.ShapeDtypeStruct((2, SUB, 4 * HD), BF16)]
-        scratch.append(pltpu.VMEM((2, SUB, 4 * HD), BF16))
     if extra:
         scratch.append(pltpu.SemaphoreType.DMA((4,)))
     return pl.pallas_call(
-        functools.partial(attend_kernel, plan, len(sources), chosen, first, last, extra),
+        functools.partial(attend_kernel, plan, early, len(sources), chosen, first, last, extra),
         out_shape=out_shape,
         in_specs=[SMEM, SMEM] + [ANY] * (len(sources) + 2 + len(state)),
         out_specs=[ANY] * len(out_shape),
         scratch_shapes=scratch,
-        compiler_params=params(),
-        cost_estimate=work(rows, (most + (8 if first else 0)) * SUB),
+        compiler_params=params(24),
+        cost_estimate=work(rows, (8 if first else most) * SUB),
         name=name,
     )(hits, table, *sources, *messages, *state)
 
@@ -554,39 +566,44 @@
     messages = (msg_a, msg_b)
     fresh = jnp.concatenate([fresh_part(msg_a), fresh_part(msg_b)], axis=0)
     fresh_other = swap(fresh)
+    ring = [(x * 2 + c, (x + 1 - 2 * c) % 4 * 2 + c) for x in range(4) for c in range(2)]
+    xc = ("x", "c")
     rest = [lax.ppermute(fresh, "x", shift(4, -k)) for k in NEIGHBOURS]
     both = (0, 1)
 
-    def step(state, plan, most, sources, name, extra=None):
-        return attend(hits, table, plan, most, sources, messages, state, both, name, extra)
-
-    state = step((), [], 0, (fresh, fresh_other), "diagonal")
+    def step(state, plan, early, most, sources, name, extra=None):
+        return attend(
+            hits, table, plan, early, most, sources, messages, state, both, name, extra
+        )
+
+    state = step((), None, None, 0, (fresh, fresh_other), "diagonal")
     own = lax.all_to_all(sent, ("s", "y"), 0, 0, tiled=True)
     own, state = lax.optimization_barrier((own, state))
+    own = jnp.concatenate([own, swap(own)], axis=0)
+    got = lax.ppermute(own, xc, ring)
+    plan = keys_at(lambda: 0, ((0, 0), (0, 16)))
     rest = jnp.concatenate(rest, axis=0)
-    left = lax.ppermute(own, "x", shift(4, 1))
-    right = lax.ppermute(own, "x", shift(4, -1))
-    plan = [keys_at(0, (0, 1)), earlier_rows((2, 3))]
-    sources = (own, swap(own), rest, swap(rest), fresh, fresh_other)
-    *state, p0, p1, p2, p3 = step(state, plan, 56, sources, "own", "route")
-    state, left, right, parts = lax.optimization_barrier((state, left, right, (p0, p1, p2, p3)))
+    early = earlier_rows(3, 4)
+    sources = (own, fresh, fresh_other, rest, swap(rest))
+    *state, p0, p1, p2, p3 = step(state, plan, early, 56, sources, "own", "route")
+    state, got, parts = lax.optimization_barrier((state, got, (p0, p1, p2, p3)))
+    got_other = swap(got)
+    far = lax.ppermute(got[:16], xc, ring)
     parts = [parts[0]] + [lax.ppermute(parts[k], "y", shift(4, k)) for k in (1, 2, 3)]
-    far_a = lax.ppermute(left[:HALF], "x", shift(4, 1))
-    far_b = lax.ppermute(right[HALF:], "x", shift(4, -1))
-    left_other, right_other = swap(left), swap(right)
-    plan = [keys_at(3, (0,)), keys_at(1, (1,))]
-    state = step(state, plan, 32, (left, right), "near")
-    state, far_a, far_b, parts = lax.optimization_barrier((state, far_a, far_b, parts))
-    far = (far_a, swap(far_a), far_b, swap(far_b))
-    *state, block = step(state, plan, 32, (left_other, right_other, *parts), "near", "join")
-    block, state, far = lax.optimization_barrier((block, state, far))
+    pieces = ((0, 0), (0, 16))
+    state = step(state, keys_at(lambda: side(True), pieces), None, 32, (got,), "near")
+    state, far, parts = lax.optimization_barrier((state, far, parts))
+    far_other = swap(far)
+    block = jnp.concatenate(parts, axis=0)
     arrived = [block] + [lax.ppermute(block, "s", shift(4, k)) for k in (1, 2, 3)]
-    plan = [keys_at(2, (0, 1, 2, 3))]
+    plan = keys_at(lambda: side(False), pieces)
+    state = step(state, plan, None, 32, (got_other,), "near")
+    state, far_other, arrived = lax.optimization_barrier((state, far_other, arrived))
+    far = (far, far_other)
+    plan = keys_at(lambda: 2, ((0, 0), (1, 0)))
     outs = []
     for r, back in ((0, back_a), (1, back_b)):
-        if r == 1:
-            arrived, state = lax.optimization_barrier((arrived, state))
-        (out,) = attend(hits, table, plan, 32, far, messages, state, (r,), "far")
+        (out,) = attend(hits, table, plan, None, 32, far, messages, state, (r,), "far")
         outs.append(lax.ppermute(out, yc, back))
     attended = by_parity(
         parity, jnp.concatenate(outs, axis=1), jnp.concatenate(outs[::-1], axis=1)

time: 119 us -> 104 us (0.87); the launches traced: 119 us -> 102 us
  Pallas kernels: 60.9 us -> 31.1 us
  starting transfers between devices: 49.6 us -> 59.6 us
  waiting for transfers between devices: 3 us -> 8.76 us
  local copies, waits for them, and re-layouts: 3.92 us -> 0.28 us
    pallas_call x6, Pallas kernels: 53 us -> 23.2 us  [attend(): pl.pallas_call(functools.partial(attend_kernel, plan, early, len(sources)...]
    ppermute x3, starting transfers between devices: 2.73 us -> 23.5 us  [shards(): lax.ppermute(block, 's', shift(4, k))]
    ppermute x4 -> x2, starting transfers between devices: 13.7 us -> 3.82 us  [the longest x1 2.55 us: shards(): got = lax.ppermute(own, xc, ring)]
    ppermute x4 -> x2, waiting for transfers between devices: 0.01 us -> 4.49 us  [the longest x1 4.49 us: shards(): got = lax.ppermute(own, xc, ring)]
    unnamed x48 -> x18, local copies, waits for them, and re-layouts: 3.85 us -> 0.12 us
    ppermute x3, starting transfers between devices: 5.36 us -> 3.82 us  [shards(): lax.ppermute(parts[k], 'y', shift(4, k))]
    ppermute x7 -> x5, starting transfers between devices: 7.27 us -> 7.69 us  [swap(): return lax.ppermute(part, 'c', shift(2, 1))]
  transfers between devices with their start and end apart: 25 -> 21, of which waited for: 1 -> 5; matrix products, arithmetic and copies ran while one was open for 0% -> 0% of each run, Pallas kernels for 49% -> 26%
where the time goes in v1:
time: 104 us; the launch traced here: 102 us
  starting transfers between devices  59.6 us (57%)
  Pallas kernels  31.1 us (30%)
  waiting for transfers between devices  8.76 us (8%)
    ppermute x3, starting transfers between devices, shards(): lax.ppermute(block, 's', shift(4, k))  23.5 us
    pallas_call x6, Pallas kernels, attend(): pl.pallas_call(functools.partial(attend_kernel, plan, early, len(sources)...  23.2 us
    ppermute x5, starting transfers between devices, swap(): return lax.ppermute(part, 'c', shift(2, 1))  7.69 us
    all_to_all x1, starting transfers between devices, shards(): own = lax.all_to_all(sent, ('s', 'y'), 0, 0, tiled=True)  5.26 us
    ppermute x2, starting transfers between devices, shards(): outs.append(lax.ppermute(out, yc, back))  4.95 us
    ppermute x1, waiting for transfers between devices, shards(): got = lax.ppermute(own, xc, ring)  4.49 us
    ppermute x3, starting transfers between devices, shards(): rest = [lax.ppermute(fresh, 'x', shift(4, -k)) for k in NEIGHBOURS]  4.22 us
    ppermute x1, starting transfers between devices, shards(): msg_b = lax.ppermute(msg_b, yc, to_b)  4.2 us
  transfers between devices with their start and end apart: 21, of which 5 were waited for; matrix products, arithmetic and copies ran while one was open for 0% of the time, Pallas kernels for 26%

profile of v1, /device:TPU:1, one launch (start us, length us, event | category | flops | bytes accessed | tf_op | source)
XLA Modules:
  0.0 101.7 jit_solution(13812721313579444166)
XLA Ops:
  0.6 2.1 %messages.1 = (bf16[1280,128]{1,0:T(8,128)(2,1)}, bf16[1280,128]{1,0:T(8,128)(2,1)}) custom-call(bf16[1,128,2048]{2,1,0:T(8,128)(2,1)} %queries.1, bf16[2,1,128,256]{3,2,1,0:T(8,128)(2,1)} %suffix.1), custom_call_target="tpu_custom_call" | custom-call | tf_op jit(solution)/shard_map/messages/pallas_call | solution.py:81
  2.8 4.2 %collective-permute-start.1 = (bf16[1280,128]{1,0:T(8,128)(2,1)}, bf16[1280,128]{1,0:T(8,128)(2,1)S(1)}, u32[]{:S(2)}, u32[]{:S(2)}) collective-permute-start(bf16[1280,128]{1,0:T(8,128)(2,1)} %get-tuple-element.48.after), channel_id=1, source_target_pairs={{0,2},{1,6},{2,0},{3,4},{4,3},{5,7},{6,1},{7,5},{8,10},{9,14},{10,... | collective-permute-start | bytes 983048 | tf_op jit(solution)/shard_map/ppermute | solution.py:565
  7.0 2.1 %collective-permute-start = (bf16[1280,128]{1,0:T(8,128)(2,1)}, bf16[1280,128]{1,0:T(8,128)(2,1)S(1)}, u32[]{:S(2)}, u32[]{:S(2)}) collective-permute-start(bf16[1280,128]{1,0:T(8,128)(2,1)} %get-tuple-element.49), channel_id=1, source_target_pairs={{0,0},{1,4},{2,2},{3,6},{4,1},{5,5},{6,3},{7,7},{8,8},{9,12},{10,1... | collective-permute-start | bytes 983048 | tf_op jit(solution)/shard_map/ppermute | solution.py:564
  9.1 2.8 %pack.1 = bf16[16,2,64,128]{3,2,1,0:T(8,128)(2,1)} custom-call(s32[4,64]{1,0:T(4,128)} %refs_1_.11, bf16[2,6,64,512]{3,2,1,0:T(8,128)(2,1)} %cache.3, bf16[1280,128]{1,0:T(8,128)(2,1)} %get-tuple-element.48.after), custom_call_target="tpu_custom_call" | custom-call | flops 34359738368 | bytes 2097152 | tf_op jit(solution)/shard_map/pack/pallas_call | solution.py:119
  11.9 5.3 %all-to-all-start = ((bf16[16,2,64,128]{3,2,1,0:T(8,128)(2,1)}), bf16[16,2,64,128]{3,2,1,0:T(8,128)(2,1)S(1)}, u32[]{:S(2)}, u32[]{:S(2)}) async-start(bf16[16,2,64,128]{3,2,1,0:T(8,128)(2,1)} %pack.1), calls=%async_computation | async-start | bytes 1048576 | tf_op jit(solution)/shard_map/all_to_all | solution.py:580
  17.2 3.1 %collective-permute-start.2 = (bf16[4,2,64,128]{3,2,1,0:T(8,128)(2,1)S(1)}, bf16[4,2,64,128]{3,2,1,0:T(8,128)(2,1)S(1)}, u32[]{:S(2)}, u32[]{:S(2)}) collective-permute-start(bf16[4,2,64,128]{3,2,1,0:T(8,128)(2,1)S(1)} %pad_maximum_fusion.refs_2_.refs_3_), channel_id=1, source_target_pairs={{0,1},{1,0},{2,3},{3,2},{4,5},{5,4},{6,7},{7,6},{8,9},{9,8},{10,11... | collective-permute-start | bytes 393224 | tf_op jit(solution)/shard_map/ppermute | solution.py:548
  20.3 1.2 %collective-permute-start.4 = (bf16[4,2,64,128]{3,2,1,0:T(8,128)(2,1)S(1)}, bf16[4,2,64,128]{3,2,1,0:T(8,128)(2,1)S(1)}, u32[]{:S(2)}, u32[]{:S(2)}) collective-permute-start(bf16[4,2,64,128]{3,2,1,0:T(8,128)(2,1)S(1)} %pad_maximum_fusion.refs_2_.refs_3_), channel_id=1, source_target_pairs={{0,8},{8,16},{16,24},{24,0},{1,9},{9,17},{17,25},{25,1},{2,10},{10... | collective-permute-start | bytes 393224 | tf_op jit(solution)/shard_map/ppermute | solution.py:571
  21.6 1.5 %collective-permute-start.5 = (bf16[4,2,64,128]{3,2,1,0:T(8,128)(2,1)S(1)}, bf16[4,2,64,128]{3,2,1,0:T(8,128)(2,1)S(1)}, u32[]{:S(2)}, u32[]{:S(2)}) collective-permute-start(bf16[4,2,64,128]{3,2,1,0:T(8,128)(2,1)S(1)} %pad_maximum_fusion.refs_2_.refs_3_), channel_id=1, source_target_pairs={{0,24},{8,0},{16,8},{24,16},{1,25},{9,1},{17,9},{25,17},{2,26},{10... | collective-permute-start | bytes 393224 | tf_op jit(solution)/shard_map/ppermute | solution.py:571
  23.0 1.5 %collective-permute-start.6 = (bf16[4,2,64,128]{3,2,1,0:T(8,128)(2,1)S(1)}, bf16[4,2,64,128]{3,2,1,0:T(8,128)(2,1)S(1)}, u32[]{:S(2)}, u32[]{:S(2)}) collective-permute-start(bf16[4,2,64,128]{3,2,1,0:T(8,128)(2,1)S(1)} %pad_maximum_fusion.refs_2_.refs_3_), channel_id=1, source_target_pairs={{0,16},{8,24},{16,0},{24,8},{1,17},{9,25},{17,1},{25,9},{2,18},{10... | collective-permute-start | bytes 393224 | tf_op jit(solution)/shard_map/ppermute | solution.py:571
  24.6 4.3 %diagonal.1 = (f32[2,8,1024]{2,1,0:T(8,128)S(1)}, f32[2,8,1024]{2,1,0:T(8,128)S(1)}, f32[2,128,1024]{2,1,0:T(8,128)S(1)}) custom-call(s32[4]{0:T(128)S(1)} %copy-done, s32[4,64]{1,0:T(4,128)S(1)} %copy-done.1, bf16[4,2,64,128]{3,2,1,0:T(8,128)(2,1)S(1)} %pad_maximum_fusion.refs_2_.refs_3_, ...), custom_call_target="tpu_custom_call" | custom-call | flops 2147483648 | bytes 2097152 | tf_op jit(solution)/shard_map/diagonal/pallas_call | solution.py:527
  28.9 1.4 %collective-permute-start.3 = (bf16[16,2,64,128]{3,2,1,0:T(8,128)(2,1)S(1)}, bf16[16,2,64,128]{3,2,1,0:T(8,128)(2,1)S(1)}, u32[]{:S(2)}, u32[]{:S(2)}) collective-permute-start(bf16[16,2,64,128]{3,2,1,0:T(8,128)(2,1)S(1)} %all-to-all-done), channel_id=1, source_target_pairs={{0,1},{1,0},{2,3},{3,2},{4,5},{5,4},{6,7},{7,6},{8,9},{9,8},{10,11... | collective-permute-start | bytes 1572872 | tf_op jit(solution)/shard_map/ppermute | solution.py:548
  30.4 0.9 collective-permute-start.7
  31.9 2.5 %collective-permute-start.8 = (bf16[32,2,64,128]{3,2,1,0:T(8,128)(2,1)S(1)}, bf16[32,2,64,128]{3,2,1,0:T(8,128)(2,1)S(1)}, u32[]{:S(2)}, u32[]{:S(2)}) collective-permute-start(bf16[32,2,64,128]{3,2,1,0:T(8,128)(2,1)S(1)} %constant_dynamic-update-slice_fusion.refs_2_), channel_id=1, source_target_pairs={{0,8},{1,25},{8,16},{9,1},{16,24},{17,9},{24,0},{25,17},{2,10},{3,... | collective-permute-start | bytes 3145736 | tf_op jit(solution)/shard_map/ppermute | solution.py:583
  34.5 7.2 %own.1 = (f32[2,8,1024]{2,1,0:T(8,128)S(1)}, f32[2,8,1024]{2,1,0:T(8,128)S(1)}, f32[2,128,1024]{2,1,0:T(8,128)S(1)}, bf16[2,64,128]{2,1,0:T(8,128)(2,1)S(1)}, bf...) custom-call(s32[4]{0:T(128)S(1)} %copy-done, ...), custom_call_target="tpu_custom_call" | custom-call | flops 15032385536 | bytes 2097152 | tf_op jit(solution)/shard_map/own/pallas_call | solution.py:527
  41.7 4.5 %collective-permute-done.8.refs_2_ = bf16[32,2,64,128]{3,2,1,0:T(8,128)(2,1)S(1)} collective-permute-done((bf16[32,2,64,128]{3,2,1,0:T(8,128)(2,1)S(1)}, bf16[32,2,64,128]{3,2,1,0:T(8,128)(2,1)S(1)}, u32[]{:S(2)}, u32[]{:S(2)}) %collective-permute-start.8) | collective-permute-done | bytes 1048608 | tf_op jit(solution)/shard_map/ppermute | solution.py:583
  46.3 2.2 %collective-permute-start.13 = (bf16[32,2,64,128]{3,2,1,0:T(8,128)(2,1)S(1)}, bf16[32,2,64,128]{3,2,1,0:T(8,128)(2,1)S(1)}, u32[]{:S(2)}, u32[]{:S(2)}) collective-permute-start(bf16[32,2,64,128]{3,2,1,0:T(8,128)(2,1)S(1)} %collective-permute-done.8.refs_2_), channel_id=1, source_target_pairs={{0,1},{1,0},{2,3},{3,2},{4,5},{5,4},{6,7},{7,6},{8,9},{9,8},{10,11... | collective-permute-start | bytes 3145736 | tf_op jit(solution)/shard_map/ppermute | solution.py:548
  48.5 1.3 %collective-permute-start.9 = (bf16[16,2,64,128]{3,2,1,0:T(8,128)(2,1)S(1)}, bf16[16,2,64,128]{3,2,1,0:T(8,128)(2,1)S(1)}, u32[]{:S(2)}, u32[]{:S(2)}) collective-permute-start(bf16[16,2,64,128]{3,2,1,0:T(8,128)(2,1)S(1)} %slice.11), channel_id=1, source_target_pairs={{0,8},{1,25},{8,16},{9,1},{16,24},{17,9},{24,0},{25,17},{2,10},{3,... | collective-permute-start | bytes 1572872 | tf_op jit(solution)/shard_map/ppermute | solution.py:591
  50.1 2.4 %collective-permute-start.11 = (bf16[2,64,128]{2,1,0:T(8,128)(2,1)S(1)}, bf16[2,64,128]{2,1,0:T(8,128)(2,1)S(1)}, u32[]{:S(2)}, u32[]{:S(2)}) collective-permute-start(bf16[2,64,128]{2,1,0:T(8,128)(2,1)S(1)} %get-tuple-element.73), channel_id=1, source_target_pairs={{0,4},{2,6},{4,0},{6,2},{1,5},{3,7},{5,1},{7,3},{8,12},{10,14},{12... | collective-permute-start | bytes 98312 | tf_op jit(solution)/shard_map/ppermute | solution.py:592
  52.4 1.2 %collective-permute-start.12 = (bf16[2,64,128]{2,1,0:T(8,128)(2,1)S(1)}, bf16[2,64,128]{2,1,0:T(8,128)(2,1)S(1)}, u32[]{:S(2)}, u32[]{:S(2)}) collective-permute-start(bf16[2,64,128]{2,1,0:T(8,128)(2,1)S(1)} %get-tuple-element.74), channel_id=1, source_target_pairs={{0,6},{2,0},{4,2},{6,4},{1,7},{3,1},{5,3},{7,5},{8,14},{10,8},{12,... | collective-permute-start | bytes 98312 | tf_op jit(solution)/shard_map/ppermute | solution.py:592
  53.6 4.1 %near.2 = (f32[2,8,1024]{2,1,0:T(8,128)S(1)}, f32[2,8,1024]{2,1,0:T(8,128)S(1)}, f32[2,128,1024]{2,1,0:T(8,128)S(1)}) custom-call(s32[4]{0:T(128)S(1)} %copy-done, s32[4,64]{1,0:T(4,128)S(1)} %copy-done.1, bf16[32,2,64,128]{3,2,1,0:T(8,128)(2,1)S(1)} %collective-permute-done.8.refs_2_, bf16[1280,128]{1,0:T(8,128)(2,1)S(1)} %collective-permute-done.refs_4_.refs_7_.refs_3_, ...), custom_call_target="tpu_custom_call" | custom-call | flops 8589934592 | bytes 2097152 | tf_op jit(solution)/shard_map/near/pallas_call | solution.py:527
  57.8 6.6 %collective-permute-start.15 = (bf16[8,64,128]{2,1,0:T(8,128)(2,1)S(1)}, bf16[8,64,128]{2,1,0:T(8,128)(2,1)S(1)}, u32[]{:S(2)}, u32[]{:S(2)}) collective-permute-start(bf16[8,64,128]{2,1,0:T(8,128)(2,1)S(1)} %constant_dynamic-update-slice_fusion.5.refs_0_), channel_id=1, source_target_pairs={{0,32},{32,64},{64,96},{96,0},{1,33},{33,65},{65,97},{97,1},{2,34}... | collective-permute-start | bytes 393224 | tf_op jit(solution)/shard_map/ppermute | solution.py:598
  64.4 14.9 %collective-permute-start.16 = (bf16[8,64,128]{2,1,0:T(8,128)(2,1)S(1)}, bf16[8,64,128]{2,1,0:T(8,128)(2,1)S(1)}, u32[]{:S(2)}, u32[]{:S(2)}) collective-permute-start(bf16[8,64,128]{2,1,0:T(8,128)(2,1)S(1)} %constant_dynamic-update-slice_fusion.5.refs_0_), channel_id=1, source_target_pairs={{0,64},{32,96},{64,0},{96,32},{1,65},{33,97},{65,1},{97,33},{2,66}... | collective-permute-start | bytes 393224 | tf_op jit(solution)/shard_map/ppermute | solution.py:598
  79.3 2.0 %collective-permute-start.17 = (bf16[8,64,128]{2,1,0:T(8,128)(2,1)S(1)}, bf16[8,64,128]{2,1,0:T(8,128)(2,1)S(1)}, u32[]{:S(2)}, u32[]{:S(2)}) collective-permute-start(bf16[8,64,128]{2,1,0:T(8,128)(2,1)S(1)} %constant_dynamic-update-slice_fusion.5.refs_0_), channel_id=1, source_target_pairs={{0,96},{32,0},{64,32},{96,64},{1,97},{33,1},{65,33},{97,65},{2,98}... | collective-permute-start | bytes 393224 | tf_op jit(solution)/shard_map/ppermute | solution.py:598
  81.3 2.2 %near.3 = (f32[2,8,1024]{2,1,0:T(8,128)S(1)}, f32[2,8,1024]{2,1,0:T(8,128)S(1)}, f32[2,128,1024]{2,1,0:T(8,128)S(1)}) custom-call(s32[4]{0:T(128)S(1)} %copy-done, s32[4,64]{1,0:T(4,128)S(1)} %copy-done.1, bf16[32,2,64,128]{3,2,1,0:T(8,128)(2,1)S(1)} %collective-permute-done.13.refs_2_, bf16[1280,128]{1,0:T(8,128)(2,1)S(1)} %collective-permute-done.refs_4_.refs_7_.refs_3_, ...), custom_call_target="tpu_custom_call" | custom-call | flops 8589934592 | bytes 2097152 | tf_op jit(solution)/shard_map/near/pallas_call | solution.py:527
  83.6 2.8 %far.2 = bf16[128,1024]{1,0:T(8,128)(2,1)S(1)} custom-call(s32[4]{0:T(128)S(1)} %copy-done, s32[4,64]{1,0:T(4,128)S(1)} %copy-done.1, bf16[16,2,64,128]{3,2,1,0:T(8,128)(2,1)S(1)} %collective-permute-done.9.refs_2_, bf16[16,2,64,128]{3,2,1,0:T(8,128)(2,1)S(1)} %collective-permute-done.14.refs_3_, ...), custom_call_target="tpu_custom_call" | custom-call | flops 4294967296 | bytes 2097152 | tf_op jit(solution)/shard_map/far/pallas_call | solution.py:527
  86.4 4.4 %collective-permute-start.18 = (bf16[128,1024]{1,0:T(8,128)(2,1)S(1)}, bf16[128,1024]{1,0:T(8,128)(2,1)S(1)}, u32[]{:S(2)}, u32[]{:S(2)}) collective-permute-start(bf16[128,1024]{1,0:T(8,128)(2,1)S(1)} %far.2), channel_id=1, source_target_pairs={{0,0},{4,1},{2,2},{6,3},{1,4},{5,5},{3,6},{7,7},{8,8},{12,9},{10,1... | collective-permute-start | bytes 786440 | tf_op jit(solution)/shard_map/ppermute | solution.py:607
  90.9 2.6 %far.3 = bf16[128,1024]{1,0:T(8,128)(2,1)S(1)} custom-call(s32[4]{0:T(128)S(1)} %copy-done, s32[4,64]{1,0:T(4,128)S(1)} %copy-done.1, bf16[16,2,64,128]{3,2,1,0:T(8,128)(2,1)S(1)} %collective-permute-done.9.refs_2_, bf16[16,2,64,128]{3,2,1,0:T(8,128)(2,1)S(1)} %collective-permute-done.14.refs_3_, ...), custom_call_target="tpu_custom_call" | custom-call | flops 4294967296 | bytes 2097152 | tf_op jit(solution)/shard_map/far/pallas_call | solution.py:527
  93.4 0.5 collective-permute-start.19
  93.9 3.1 %place.1 = bf16[2,6,64,512]{3,2,1,0:T(8,128)(2,1)} custom-call(s32[4]{0:T(128)} %hits.1, s32[4,16]{1,0:T(4,128)} %dests.1, bf16[2,6,64,512]{3,2,1,0:T(8,128)(2,1)} %cache.3, bf16[8,64,128]{2,1,0:T(8,128)(2,1)} %copy-done.2, bf16[8,64,128]{2,1,0:T(8,128)(2,1)} %copy-done.3, bf16[8,64,128]{2,1,0:T(8,128)(2,1)} %copy-done.4, bf16[8,64,128]{2,1,0:T(8,128)(2,1)} %copy-done.5), custom_call_target="tpu_custom_call" | custom-call | tf_op jit(solution)/shard_map/place/pallas_call | solution.py:162
  97.0 1.0 collective-permute-done.18
  98.0 2.8 %collective-permute-done.19 = bf16[128,1024]{1,0:T(8,128)(2,1)S(1)} collective-permute-done((bf16[128,1024]{1,0:T(8,128)(2,1)S(1)}, bf16[128,1024]{1,0:T(8,128)(2,1)S(1)}, u32[]{:S(2)}, u32[]{:S(2)}) %collective-permute-start.19) | collective-permute-done | bytes 262176 | tf_op jit(solution)/shard_map/ppermute | solution.py:607
  100.8 0.9 maximum_select_fusion
  (45 shorter events, 1.1 us)
Async XLA Ops:
  2.8 14.4 %collective-permute-start.1 = (bf16[1280,128]{1,0:T(8,128)(2,1)}, bf16[1280,128]{1,0:T(8,128)(2,1)S(1)}, u32[]{:S(2)}, u32[]{:S(2)}) collective-permute-start(bf16[1280,128]{1,0:T(8,128)(2,1)} %get-tuple-element.48.after), channel_id=1, source_target_pairs={{0,2},{1,6},{2,0},{3,4},{4,3},{5,7},{6,1},{7,5},{8,10},{9,14},{10,... | collective-permute-start | bytes 983048 | tf_op jit(solution)/shard_map/ppermute | solution.py:565
  7.0 10.2 %collective-permute-start = (bf16[1280,128]{1,0:T(8,128)(2,1)}, bf16[1280,128]{1,0:T(8,128)(2,1)S(1)}, u32[]{:S(2)}, u32[]{:S(2)}) collective-permute-start(bf16[1280,128]{1,0:T(8,128)(2,1)} %get-tuple-element.49), channel_id=1, source_target_pairs={{0,0},{1,4},{2,2},{3,6},{4,1},{5,5},{6,3},{7,7},{8,8},{9,12},{10,1... | collective-permute-start | bytes 983048 | tf_op jit(solution)/shard_map/ppermute | solution.py:564
  11.9 17.1 %all-to-all-start = ((bf16[16,2,64,128]{3,2,1,0:T(8,128)(2,1)}), bf16[16,2,64,128]{3,2,1,0:T(8,128)(2,1)S(1)}, u32[]{:S(2)}, u32[]{:S(2)}) async-start(bf16[16,2,64,128]{3,2,1,0:T(8,128)(2,1)} %pack.1), calls=%async_computation | async-start | bytes 1048576 | tf_op jit(solution)/shard_map/all_to_all | solution.py:580
  17.2 7.4 %copy-start = (s32[4]{0:T(128)S(1)}, s32[4]{0:T(128)}, u32[]{:S(2)}) copy-start(s32[4]{0:T(128)} %hits.1) | copy-start | bytes 52
  17.2 7.4 %copy-start.1 = (s32[4,64]{1,0:T(4,128)S(1)}, s32[4,64]{1,0:T(4,128)}, u32[]{:S(2)}) copy-start(s32[4,64]{1,0:T(4,128)} %refs_1_.11) | copy-start | bytes 3076
  17.2 7.4 %collective-permute-start.2 = (bf16[4,2,64,128]{3,2,1,0:T(8,128)(2,1)S(1)}, bf16[4,2,64,128]{3,2,1,0:T(8,128)(2,1)S(1)}, u32[]{:S(2)}, u32[]{:S(2)}) collective-permute-start(bf16[4,2,64,128]{3,2,1,0:T(8,128)(2,1)S(1)} %pad_maximum_fusion.refs_2_.refs_3_), channel_id=1, source_target_pairs={{0,1},{1,0},{2,3},{3,2},{4,5},{5,4},{6,7},{7,6},{8,9},{9,8},{10,11... | collective-permute-start | bytes 393224 | tf_op jit(solution)/shard_map/ppermute | solution.py:548
  20.3 10.0 %collective-permute-start.4 = (bf16[4,2,64,128]{3,2,1,0:T(8,128)(2,1)S(1)}, bf16[4,2,64,128]{3,2,1,0:T(8,128)(2,1)S(1)}, u32[]{:S(2)}, u32[]{:S(2)}) collective-permute-start(bf16[4,2,64,128]{3,2,1,0:T(8,128)(2,1)S(1)} %pad_maximum_fusion.refs_2_.refs_3_), channel_id=1, source_target_pairs={{0,8},{8,16},{16,24},{24,0},{1,9},{9,17},{17,25},{25,1},{2,10},{10... | collective-permute-start | bytes 393224 | tf_op jit(solution)/shard_map/ppermute | solution.py:571
  21.6 8.8 %collective-permute-start.5 = (bf16[4,2,64,128]{3,2,1,0:T(8,128)(2,1)S(1)}, bf16[4,2,64,128]{3,2,1,0:T(8,128)(2,1)S(1)}, u32[]{:S(2)}, u32[]{:S(2)}) collective-permute-start(bf16[4,2,64,128]{3,2,1,0:T(8,128)(2,1)S(1)} %pad_maximum_fusion.refs_2_.refs_3_), channel_id=1, source_target_pairs={{0,24},{8,0},{16,8},{24,16},{1,25},{9,1},{17,9},{25,17},{2,26},{10... | collective-permute-start | bytes 393224 | tf_op jit(solution)/shard_map/ppermute | solution.py:571
  23.0 7.4 %collective-permute-start.6 = (bf16[4,2,64,128]{3,2,1,0:T(8,128)(2,1)S(1)}, bf16[4,2,64,128]{3,2,1,0:T(8,128)(2,1)S(1)}, u32[]{:S(2)}, u32[]{:S(2)}) collective-permute-start(bf16[4,2,64,128]{3,2,1,0:T(8,128)(2,1)S(1)} %pad_maximum_fusion.refs_2_.refs_3_), channel_id=1, source_target_pairs={{0,16},{8,24},{16,0},{24,8},{1,17},{9,25},{17,1},{25,9},{2,18},{10... | collective-permute-start | bytes 393224 | tf_op jit(solution)/shard_map/ppermute | solution.py:571
  28.9 2.9 %collective-permute-start.3 = (bf16[16,2,64,128]{3,2,1,0:T(8,128)(2,1)S(1)}, bf16[16,2,64,128]{3,2,1,0:T(8,128)(2,1)S(1)}, u32[]{:S(2)}, u32[]{:S(2)}) collective-permute-start(bf16[16,2,64,128]{3,2,1,0:T(8,128)(2,1)S(1)} %all-to-all-done), channel_id=1, source_target_pairs={{0,1},{1,0},{2,3},{3,2},{4,5},{5,4},{6,7},{7,6},{8,9},{9,8},{10,11... | collective-permute-start | bytes 1572872 | tf_op jit(solution)/shard_map/ppermute | solution.py:548
  30.4 4.0 %collective-permute-start.7 = (bf16[12,2,64,128]{3,2,1,0:T(8,128)(2,1)S(1)}, bf16[12,2,64,128]{3,2,1,0:T(8,128)(2,1)S(1)}, u32[]{:S(2)}, u32[]{:S(2)}) collective-permute-start(bf16[12,2,64,128]{3,2,1,0:T(8,128)(2,1)S(1)} %constant_dynamic-update-slice_fusion.2.refs_5_), channel_id=1, source_target_pairs={{0,1},{1,0},{2,3},{3,2},{4,5},{5,4},{6,7},{7,6},{8,9},{9,8},{10,11... | collective-permute-start | bytes 1179656 | tf_op jit(solution)/shard_map/ppermute | solution.py:548
  31.9 14.3 %collective-permute-start.8 = (bf16[32,2,64,128]{3,2,1,0:T(8,128)(2,1)S(1)}, bf16[32,2,64,128]{3,2,1,0:T(8,128)(2,1)S(1)}, u32[]{:S(2)}, u32[]{:S(2)}) collective-permute-start(bf16[32,2,64,128]{3,2,1,0:T(8,128)(2,1)S(1)} %constant_dynamic-update-slice_fusion.refs_2_), channel_id=1, source_target_pairs={{0,8},{1,25},{8,16},{9,1},{16,24},{17,9},{24,0},{25,17},{2,10},{3,... | collective-permute-start | bytes 3145736 | tf_op jit(solution)/shard_map/ppermute | solution.py:583
  46.3 35.1 %collective-permute-start.13 = (bf16[32,2,64,128]{3,2,1,0:T(8,128)(2,1)S(1)}, bf16[32,2,64,128]{3,2,1,0:T(8,128)(2,1)S(1)}, u32[]{:S(2)}, u32[]{:S(2)}) collective-permute-start(bf16[32,2,64,128]{3,2,1,0:T(8,128)(2,1)S(1)} %collective-permute-done.8.refs_2_), channel_id=1, source_target_pairs={{0,1},{1,0},{2,3},{3,2},{4,5},{5,4},{6,7},{7,6},{8,9},{9,8},{10,11... | collective-permute-start | bytes 3145736 | tf_op jit(solution)/shard_map/ppermute | solution.py:548
  48.5 9.2 %collective-permute-start.9 = (bf16[16,2,64,128]{3,2,1,0:T(8,128)(2,1)S(1)}, bf16[16,2,64,128]{3,2,1,0:T(8,128)(2,1)S(1)}, u32[]{:S(2)}, u32[]{:S(2)}) collective-permute-start(bf16[16,2,64,128]{3,2,1,0:T(8,128)(2,1)S(1)} %slice.11), channel_id=1, source_target_pairs={{0,8},{1,25},{8,16},{9,1},{16,24},{17,9},{24,0},{25,17},{2,10},{3,... | collective-permute-start | bytes 1572872 | tf_op jit(solution)/shard_map/ppermute | solution.py:591
  49.8 7.9 %collective-permute-start.10 = (bf16[2,64,128]{2,1,0:T(8,128)(2,1)S(1)}, bf16[2,64,128]{2,1,0:T(8,128)(2,1)S(1)}, u32[]{:S(2)}, u32[]{:S(2)}) collective-permute-start(bf16[2,64,128]{2,1,0:T(8,128)(2,1)S(1)} %get-tuple-element.72), channel_id=1, source_target_pairs={{0,2},{2,4},{4,6},{6,0},{1,3},{3,5},{5,7},{7,1},{8,10},{10,12},{12... | collective-permute-start | bytes 98312 | tf_op jit(solution)/shard_map/ppermute | solution.py:592
  50.1 7.6 %collective-permute-start.11 = (bf16[2,64,128]{2,1,0:T(8,128)(2,1)S(1)}, bf16[2,64,128]{2,1,0:T(8,128)(2,1)S(1)}, u32[]{:S(2)}, u32[]{:S(2)}) collective-permute-start(bf16[2,64,128]{2,1,0:T(8,128)(2,1)S(1)} %get-tuple-element.73), channel_id=1, source_target_pairs={{0,4},{2,6},{4,0},{6,2},{1,5},{3,7},{5,1},{7,3},{8,12},{10,14},{12... | collective-permute-start | bytes 98312 | tf_op jit(solution)/shard_map/ppermute | solution.py:592
  52.4 5.3 %collective-permute-start.12 = (bf16[2,64,128]{2,1,0:T(8,128)(2,1)S(1)}, bf16[2,64,128]{2,1,0:T(8,128)(2,1)S(1)}, u32[]{:S(2)}, u32[]{:S(2)}) collective-permute-start(bf16[2,64,128]{2,1,0:T(8,128)(2,1)S(1)} %get-tuple-element.74), channel_id=1, source_target_pairs={{0,6},{2,0},{4,2},{6,4},{1,7},{3,1},{5,3},{7,5},{8,14},{10,8},{12,... | collective-permute-start | bytes 98312 | tf_op jit(solution)/shard_map/ppermute | solution.py:592
  57.8 25.8 %copy-start.2 = (bf16[8,64,128]{2,1,0:T(8,128)(2,1)}, bf16[8,64,128]{2,1,0:T(8,128)(2,1)S(1)}, u32[]{:S(2)}) copy-start(bf16[8,64,128]{2,1,0:T(8,128)(2,1)S(1)} %constant_dynamic-update-slice_fusion.5.refs_0_) | copy-start | bytes 393220
  57.8 25.8 %collective-permute-start.15 = (bf16[8,64,128]{2,1,0:T(8,128)(2,1)S(1)}, bf16[8,64,128]{2,1,0:T(8,128)(2,1)S(1)}, u32[]{:S(2)}, u32[]{:S(2)}) collective-permute-start(bf16[8,64,128]{2,1,0:T(8,128)(2,1)S(1)} %constant_dynamic-update-slice_fusion.5.refs_0_), channel_id=1, source_target_pairs={{0,32},{32,64},{64,96},{96,0},{1,33},{33,65},{65,97},{97,1},{2,34}... | collective-permute-start | bytes 393224 | tf_op jit(solution)/shard_map/ppermute | solution.py:598
  64.4 19.1 %collective-permute-start.16 = (bf16[8,64,128]{2,1,0:T(8,128)(2,1)S(1)}, bf16[8,64,128]{2,1,0:T(8,128)(2,1)S(1)}, u32[]{:S(2)}, u32[]{:S(2)}) collective-permute-start(bf16[8,64,128]{2,1,0:T(8,128)(2,1)S(1)} %constant_dynamic-update-slice_fusion.5.refs_0_), channel_id=1, source_target_pairs={{0,64},{32,96},{64,0},{96,32},{1,65},{33,97},{65,1},{97,33},{2,66}... | collective-permute-start | bytes 393224 | tf_op jit(solution)/shard_map/ppermute | solution.py:598
  79.3 4.2 %collective-permute-start.17 = (bf16[8,64,128]{2,1,0:T(8,128)(2,1)S(1)}, bf16[8,64,128]{2,1,0:T(8,128)(2,1)S(1)}, u32[]{:S(2)}, u32[]{:S(2)}) collective-permute-start(bf16[8,64,128]{2,1,0:T(8,128)(2,1)S(1)} %constant_dynamic-update-slice_fusion.5.refs_0_), channel_id=1, source_target_pairs={{0,96},{32,0},{64,32},{96,64},{1,97},{33,1},{65,33},{97,65},{2,98}... | collective-permute-start | bytes 393224 | tf_op jit(solution)/shard_map/ppermute | solution.py:598
  81.3 2.3 %collective-permute-start.14 = (bf16[16,2,64,128]{3,2,1,0:T(8,128)(2,1)S(1)}, bf16[16,2,64,128]{3,2,1,0:T(8,128)(2,1)S(1)}, u32[]{:S(2)}, u32[]{:S(2)}) collective-permute-start(bf16[16,2,64,128]{3,2,1,0:T(8,128)(2,1)S(1)} %collective-permute-done.9.refs_2_), channel_id=1, source_target_pairs={{0,1},{1,0},{2,3},{3,2},{4,5},{5,4},{6,7},{7,6},{8,9},{9,8},{10,11... | collective-permute-start | bytes 1572872 | tf_op jit(solution)/shard_map/ppermute | solution.py:548
  83.6 2.8 %copy-start.3 = (bf16[8,64,128]{2,1,0:T(8,128)(2,1)}, bf16[8,64,128]{2,1,0:T(8,128)(2,1)S(1)}, u32[]{:S(2)}) copy-start(bf16[8,64,128]{2,1,0:T(8,128)(2,1)S(1)} %collective-permute-done.15.refs_1_) | copy-start | bytes 393220
  83.6 2.8 %copy-start.4 = (bf16[8,64,128]{2,1,0:T(8,128)(2,1)}, bf16[8,64,128]{2,1,0:T(8,128)(2,1)S(1)}, u32[]{:S(2)}) copy-start(bf16[8,64,128]{2,1,0:T(8,128)(2,1)S(1)} %collective-permute-done.16.refs_2_) | copy-start | bytes 393220
  83.6 2.8 %copy-start.5 = (bf16[8,64,128]{2,1,0:T(8,128)(2,1)}, bf16[8,64,128]{2,1,0:T(8,128)(2,1)S(1)}, u32[]{:S(2)}) copy-start(bf16[8,64,128]{2,1,0:T(8,128)(2,1)S(1)} %collective-permute-done.17.refs_3_) | copy-start | bytes 393220
  86.4 11.6 %collective-permute-start.18 = (bf16[128,1024]{1,0:T(8,128)(2,1)S(1)}, bf16[128,1024]{1,0:T(8,128)(2,1)S(1)}, u32[]{:S(2)}, u32[]{:S(2)}) collective-permute-start(bf16[128,1024]{1,0:T(8,128)(2,1)S(1)} %far.2), channel_id=1, source_target_pairs={{0,0},{4,1},{2,2},{6,3},{1,4},{5,5},{3,6},{7,7},{8,8},{12,9},{10,1... | collective-permute-start | bytes 786440 | tf_op jit(solution)/shard_map/ppermute | solution.py:607
  93.4 7.3 %collective-permute-start.19 = (bf16[128,1024]{1,0:T(8,128)(2,1)S(1)}, bf16[128,1024]{1,0:T(8,128)(2,1)S(1)}, u32[]{:S(2)}, u32[]{:S(2)}) collective-permute-start(bf16[128,1024]{1,0:T(8,128)(2,1)S(1)} %far.3), channel_id=1, source_target_pairs={{2,0},{6,1},{0,2},{4,3},{3,4},{7,5},{1,6},{5,7},{10,8},{14,9},{8,1... | collective-permute-start | bytes 786440 | tf_op jit(solution)/shard_map/ppermute | solution.py:607

commit v2 on v1

--- a/solution.py
+++ b/solution.py
@@ -48,8 +48,8 @@
         else:
             pl.when(when)(lambda: one.start(priority=1))
 
-    def wait(self):
-        for one, when in self.all:
+    def wait(self, *which):
+        for one, when in [self.all[i] for i in which] or self.all:
             if when is None:
                 one.wait()
             else:
@@ -58,23 +58,26 @@
 
 def messages_kernel(queries, suffix, to_a, to_b, q, f, sems):
     _, _, my_y, _ = position()
-    copies = Copies(sems)
-    copies.start(suffix.at[:, 0], f)
-    copies.start(queries.at[0], q)
-    copies.wait()
-    copies = Copies(sems)
+    loads = Copies(sems)
+    loads.start(suffix.at[:, 0], f)
+    for order in range(2):
+        cols = pl.ds(pl.multiple_of((my_y + order) % 2 * ROWS, ROWS), ROWS)
+        loads.start(queries.at[0, :, cols], q.at[order])
+    stores = Copies(sems.at[pl.ds(3, 24)])
+    loads.wait(0)
     for order, message in enumerate((to_a, to_b)):
-        key_head = (my_y + order) % 2
+        cols = pl.ds(pl.multiple_of((my_y + order) % 2 * HD, HD), HD)
         for half in range(2):
-            cols = pl.ds(pl.multiple_of(key_head * HD, HD), HD)
             rows = pl.ds(half * SUB, SUB)
             for which in range(2):
                 at = pl.ds(ROWS + (half * 2 + which) * SUB, SUB)
-                copies.start(f.at[which, rows, cols], message.at[at])
+                stores.start(f.at[which, rows, cols], message.at[at])
+    for order, message in enumerate((to_a, to_b)):
+        loads.wait(1 + order)
         for head in range(8):
-            cols = pl.ds(pl.multiple_of(key_head * ROWS + head * HD, HD), HD)
-            copies.start(q.at[:, cols], message.at[pl.ds(head * HD, HD)])
-    copies.wait()
+            cols = pl.ds(head * HD, HD)
+            stores.start(q.at[order, :, cols], message.at[pl.ds(head * HD, HD)])
+    stores.wait()
 
 
 def make_messages(queries, suffix):
@@ -84,9 +87,9 @@
         in_specs=[ANY, ANY],
         out_specs=[ANY] * 2,
         scratch_shapes=[
-            pltpu.VMEM(queries.shape[1:], BF16),
+            pltpu.VMEM((2, HD, ROWS), BF16),
             pltpu.VMEM((2,) + suffix.shape[2:], BF16),
-            pltpu.SemaphoreType.DMA((24,)),
+            pltpu.SemaphoreType.DMA((27,)),
         ],
         compiler_params=params(),
         name="messages",
@@ -99,20 +102,20 @@
     column = my_x * 4 + my_y
     device = my_store * 16 + column
     slots = cache.shape[1]
-    copies = Copies(sems)
+    loads = Copies(sems)
     for request in range(4):
         slot = jnp.int32(0)
         for turn in range(4):
             entry = table[request, column + 16 * turn]
             slot = jnp.where(entry // slots == device, entry % slots, slot)
-        copies.start(cache.at[:, slot], blocks.at[request])
-    copies.wait()
-    copies = Copies(sems)
+        loads.start(cache.at[:, slot], blocks.at[request])
+    stores = Copies(sems.at[pl.ds(4, 16)])
     for request in range(4):
+        loads.wait(request)
         for head in range(4):
             cols = pl.ds(head * HD, HD)
-            copies.start(blocks.at[request, :, :, cols], sent.at[request * 4 + head])
-    copies.wait()
+            stores.start(blocks.at[request, :, :, cols], sent.at[request * 4 + head])
+    stores.wait()
 
 
 def pack(table, cache, after):
@@ -123,7 +126,7 @@
         out_specs=ANY,
         scratch_shapes=[
             pltpu.VMEM((4, 2, SUB, 4 * HD), BF16),
-            pltpu.SemaphoreType.DMA((16,)),
+            pltpu.SemaphoreType.DMA((20,)),
         ],
         compiler_params=params(),
         cost_estimate=work(2, 8 * TILE * SUB),
@@ -316,6 +319,7 @@
     refs = refs[:n_outs] + refs[n_outs + n_moved :]
     outs = refs[:n_outs]
     m, l, acc, q, kv, sems, more, stored = refs[n_outs : n_outs + 8]
+    room = kv.shape[0]
     refs = refs[n_outs + 8 :]
     state = (m, l, acc)
     _, _, my_y, my_core = position()
@@ -405,6 +409,7 @@
     tiles = count // TILE
     done = tiles * TILE
     half = (count - done) // SMALL
+    most_bigs = room // (2 * TILE) if last else 0
     rest = done + half * SMALL
 
     for i in range(rows):
@@ -426,7 +431,21 @@
             tile(i, shifted_fold, t * TILE, TILE, False)
             return 0
 
-        lax.fori_loop(0, tiles, full, 0)
+        lead = jnp.where(tiles > 0, 1, 0)
+        bigs = (tiles - lead) // 2 if most_bigs else 0
+
+        def big(b, _):
+            begin = (lead + 2 * b) * TILE
+            arrive(begin, begin + 2 * TILE)
+            tile(i, shifted_fold, begin, 2 * TILE, False)
+            return 0
+
+        if most_bigs:
+            lax.fori_loop(0, lead, full, 0)
+            lax.fori_loop(0, bigs, big, 0)
+            lax.fori_loop(lead + 2 * bigs, tiles, full, 0)
+        else:
+            lax.fori_loop(0, tiles, full, 0)
 
         @pl.when(half > 0)
         def _():
@@ -596,14 +615,20 @@
     far_other = swap(far)
     block = jnp.concatenate(parts, axis=0)
     arrived = [block] + [lax.ppermute(block, "s", shift(4, k)) for k in (1, 2, 3)]
-    plan = keys_at(lambda: side(False), pieces)
-    state = step(state, plan, None, 32, (got_other,), "near")
-    state, far_other, arrived = lax.optimization_barrier((state, far_other, arrived))
     far = (far, far_other)
-    plan = keys_at(lambda: 2, ((0, 0), (1, 0)))
+    sources = (got_other, *far)
+    plans = [keys_at(lambda: side(False), pieces), keys_at(lambda: 2, ((1, 0), (2, 0)))]
+
+    def plan(hits, table, refs, fetch, slot):
+        for one in plans:
+            slot = one(hits, table, refs, fetch, slot)
+        return slot
+
     outs = []
     for r, back in ((0, back_a), (1, back_b)):
-        (out,) = attend(hits, table, plan, None, 32, far, messages, state, (r,), "far")
+        if r == 1:
+            arrived, state, _ = lax.optimization_barrier((arrived, state, out))
+        (out,) = attend(hits, table, plan, None, 64, sources, messages, state, (r,), "far")
         outs.append(lax.ppermute(out, yc, back))
     attended = by_parity(
         parity, jnp.concatenate(outs, axis=1), jnp.concatenate(outs[::-1], axis=1)

time: 104 us -> 105 us (level)
  the two profiles are of different devices: /device:TPU:1 before, /device:TPU:5 now
where the time goes in v2:
time: 105 us; the launch traced here: 103 us
  starting transfers between devices  54 us (51%)
  Pallas kernels  34 us (32%)
  waiting for transfers between devices  12.9 us (12%)
    pallas_call x5, Pallas kernels, attend(): pl.pallas_call(functools.partial(attend_kernel, plan, early, len(sources)...  26.3 us
    ppermute x3, starting transfers between devices, shards(): lax.ppermute(block, 's', shift(4, k))  19.7 us
    ppermute x5, starting transfers between devices, swap(): return lax.ppermute(part, 'c', shift(2, 1))  11.6 us
    ppermute x1, waiting for transfers between devices, shards(): got = lax.ppermute(own, xc, ring)  7.24 us
    all_to_all x1, starting transfers between devices, shards(): own = lax.all_to_all(sent, ('s', 'y'), 0, 0, tiled=True)  5.26 us
    ppermute x2, starting transfers between devices, shards(): outs.append(lax.ppermute(out, yc, back))  4.33 us
    ppermute x3, starting transfers between devices, shards(): lax.ppermute(parts[k], 'y', shift(4, k))  4.09 us
    ppermute x1, starting transfers between devices, shards(): msg_b = lax.ppermute(msg_b, yc, to_b)  3.37 us
  transfers between devices with their start and end apart: 21, of which 5 were waited for; matrix products, arithmetic and copies ran while one was open for 0% of the time, Pallas kernels for 25%

profile of v2, /device:TPU:5, one launch (start us, length us, event | category | flops | bytes accessed | tf_op | source)
XLA Modules:
  0.0 103.2 jit_solution(3207146137377394381)
XLA Ops:
  0.6 2.0 %messages.1 = (bf16[1280,128]{1,0:T(8,128)(2,1)}, bf16[1280,128]{1,0:T(8,128)(2,1)}) custom-call(bf16[1,128,2048]{2,1,0:T(8,128)(2,1)} %queries.1, bf16[2,1,128,256]{3,2,1,0:T(8,128)(2,1)} %suffix.1), custom_call_target="tpu_custom_call" | custom-call | tf_op jit(solution)/shard_map/messages/pallas_call | solution.py:84
  2.7 3.4 %collective-permute-start.1 = (bf16[1280,128]{1,0:T(8,128)(2,1)}, bf16[1280,128]{1,0:T(8,128)(2,1)S(1)}, u32[]{:S(2)}, u32[]{:S(2)}) collective-permute-start(bf16[1280,128]{1,0:T(8,128)(2,1)} %get-tuple-element.44.after), channel_id=1, source_target_pairs={{0,2},{1,6},{2,0},{3,4},{4,3},{5,7},{6,1},{7,5},{8,10},{9,14},{10,... | collective-permute-start | bytes 983048 | tf_op jit(solution)/shard_map/ppermute | solution.py:584
  6.0 2.1 %collective-permute-start = (bf16[1280,128]{1,0:T(8,128)(2,1)}, bf16[1280,128]{1,0:T(8,128)(2,1)S(1)}, u32[]{:S(2)}, u32[]{:S(2)}) collective-permute-start(bf16[1280,128]{1,0:T(8,128)(2,1)} %get-tuple-element.45), channel_id=1, source_target_pairs={{0,0},{1,4},{2,2},{3,6},{4,1},{5,5},{6,3},{7,7},{8,8},{9,12},{10,1... | collective-permute-start | bytes 983048 | tf_op jit(solution)/shard_map/ppermute | solution.py:583
  8.1 2.7 %pack.1 = bf16[16,2,64,128]{3,2,1,0:T(8,128)(2,1)} custom-call(s32[4,64]{1,0:T(4,128)} %refs_1_.9, bf16[2,6,64,512]{3,2,1,0:T(8,128)(2,1)} %cache.3, bf16[1280,128]{1,0:T(8,128)(2,1)} %get-tuple-element.44.after), custom_call_target="tpu_custom_call" | custom-call | flops 34359738368 | bytes 2097152 | tf_op jit(solution)/shard_map/pack/pallas_call | solution.py:122
  10.8 5.3 %all-to-all-start = ((bf16[16,2,64,128]{3,2,1,0:T(8,128)(2,1)}), bf16[16,2,64,128]{3,2,1,0:T(8,128)(2,1)S(1)}, u32[]{:S(2)}, u32[]{:S(2)}) async-start(bf16[16,2,64,128]{3,2,1,0:T(8,128)(2,1)} %pack.1), calls=%async_computation | async-start | bytes 1048576 | tf_op jit(solution)/shard_map/all_to_all | solution.py:599
  16.2 3.1 %collective-permute-start.2 = (bf16[4,2,64,128]{3,2,1,0:T(8,128)(2,1)S(1)}, bf16[4,2,64,128]{3,2,1,0:T(8,128)(2,1)S(1)}, u32[]{:S(2)}, u32[]{:S(2)}) collective-permute-start(bf16[4,2,64,128]{3,2,1,0:T(8,128)(2,1)S(1)} %pad_maximum_fusion.refs_2_.refs_3_), channel_id=1, source_target_pairs={{0,1},{1,0},{2,3},{3,2},{4,5},{5,4},{6,7},{7,6},{8,9},{9,8},{10,11... | collective-permute-start | bytes 393224 | tf_op jit(solution)/shard_map/ppermute | solution.py:567
  19.3 0.9 collective-permute-start.4
  20.2 0.5 collective-permute-start.5
  20.8 1.4 %collective-permute-start.6 = (bf16[4,2,64,128]{3,2,1,0:T(8,128)(2,1)S(1)}, bf16[4,2,64,128]{3,2,1,0:T(8,128)(2,1)S(1)}, u32[]{:S(2)}, u32[]{:S(2)}) collective-permute-start(bf16[4,2,64,128]{3,2,1,0:T(8,128)(2,1)S(1)} %pad_maximum_fusion.refs_2_.refs_3_), channel_id=1, source_target_pairs={{0,16},{8,24},{16,0},{24,8},{1,17},{9,25},{17,1},{25,9},{2,18},{10... | collective-permute-start | bytes 393224 | tf_op jit(solution)/shard_map/ppermute | solution.py:590
  22.2 4.3 %diagonal.1 = (f32[2,8,1024]{2,1,0:T(8,128)S(1)}, f32[2,8,1024]{2,1,0:T(8,128)S(1)}, f32[2,128,1024]{2,1,0:T(8,128)S(1)}) custom-call(s32[4]{0:T(128)S(1)} %copy-done, s32[4,64]{1,0:T(4,128)S(1)} %copy-done.1, bf16[4,2,64,128]{3,2,1,0:T(8,128)(2,1)S(1)} %pad_maximum_fusion.refs_2_.refs_3_, ...), custom_call_target="tpu_custom_call" | custom-call | flops 2147483648 | bytes 2097152 | tf_op jit(solution)/shard_map/diagonal/pallas_call | solution.py:546
  26.6 2.7 %collective-permute-start.3 = (bf16[16,2,64,128]{3,2,1,0:T(8,128)(2,1)S(1)}, bf16[16,2,64,128]{3,2,1,0:T(8,128)(2,1)S(1)}, u32[]{:S(2)}, u32[]{:S(2)}) collective-permute-start(bf16[16,2,64,128]{3,2,1,0:T(8,128)(2,1)S(1)} %all-to-all-done), channel_id=1, source_target_pairs={{0,1},{1,0},{2,3},{3,2},{4,5},{5,4},{6,7},{7,6},{8,9},{9,8},{10,11... | collective-permute-start | bytes 1572872 | tf_op jit(solution)/shard_map/ppermute | solution.py:567
  29.5 1.3 %collective-permute-done.3 = bf16[16,2,64,128]{3,2,1,0:T(8,128)(2,1)S(1)} collective-permute-done((bf16[16,2,64,128]{3,2,1,0:T(8,128)(2,1)S(1)}, bf16[16,2,64,128]{3,2,1,0:T(8,128)(2,1)S(1)}, u32[]{:S(2)}, u32[]{:S(2)}) %collective-permute-start.3) | collective-permute-done | bytes 524320 | tf_op jit(solution)/shard_map/ppermute | solution.py:567
  30.9 0.3 collective-permute-start.8
  31.2 0.2 collective-permute-done.7.refs_6_
  31.4 6.3 %own.1 = (f32[2,8,1024]{2,1,0:T(8,128)S(1)}, f32[2,8,1024]{2,1,0:T(8,128)S(1)}, f32[2,128,1024]{2,1,0:T(8,128)S(1)}, bf16[2,64,128]{2,1,0:T(8,128)(2,1)S(1)}, bf...) custom-call(s32[4]{0:T(128)S(1)} %copy-done, ...), custom_call_target="tpu_custom_call" | custom-call | flops 15032385536 | bytes 2097152 | tf_op jit(solution)/shard_map/own/pallas_call | solution.py:546
  37.7 7.2 %collective-permute-done.8.refs_2_ = bf16[32,2,64,128]{3,2,1,0:T(8,128)(2,1)S(1)} collective-permute-done((bf16[32,2,64,128]{3,2,1,0:T(8,128)(2,1)S(1)}, bf16[32,2,64,128]{3,2,1,0:T(8,128)(2,1)S(1)}, u32[]{:S(2)}, u32[]{:S(2)}) %collective-permute-start.8) | collective-permute-done | bytes 1048608 | tf_op jit(solution)/shard_map/ppermute | solution.py:602
  44.9 1.2 %collective-permute-start.9 = (bf16[32,2,64,128]{3,2,1,0:T(8,128)(2,1)S(1)}, bf16[32,2,64,128]{3,2,1,0:T(8,128)(2,1)S(1)}, u32[]{:S(2)}, u32[]{:S(2)}) collective-permute-start(bf16[32,2,64,128]{3,2,1,0:T(8,128)(2,1)S(1)} %collective-permute-done.8.refs_2_), channel_id=1, source_target_pairs={{0,1},{1,0},{2,3},{3,2},{4,5},{5,4},{6,7},{7,6},{8,9},{9,8},{10,11... | collective-permute-start | bytes 3145736 | tf_op jit(solution)/shard_map/ppermute | solution.py:567
  46.2 0.3 collective-permute-start.10
  46.5 0.5 collective-permute-start.11
  47.0 2.4 %collective-permute-start.12 = (bf16[2,64,128]{2,1,0:T(8,128)(2,1)S(1)}, bf16[2,64,128]{2,1,0:T(8,128)(2,1)S(1)}, u32[]{:S(2)}, u32[]{:S(2)}) collective-permute-start(bf16[2,64,128]{2,1,0:T(8,128)(2,1)S(1)} %get-tuple-element.69), channel_id=1, source_target_pairs={{0,4},{2,6},{4,0},{6,2},{1,5},{3,7},{5,1},{7,3},{8,12},{10,14},{12... | collective-permute-start | bytes 98312 | tf_op jit(solution)/shard_map/ppermute | solution.py:611
  49.4 1.2 %collective-permute-start.13 = (bf16[2,64,128]{2,1,0:T(8,128)(2,1)S(1)}, bf16[2,64,128]{2,1,0:T(8,128)(2,1)S(1)}, u32[]{:S(2)}, u32[]{:S(2)}) collective-permute-start(bf16[2,64,128]{2,1,0:T(8,128)(2,1)S(1)} %get-tuple-element.70), channel_id=1, source_target_pairs={{0,6},{2,0},{4,2},{6,4},{1,7},{3,1},{5,3},{7,5},{8,14},{10,8},{12,... | collective-permute-start | bytes 98312 | tf_op jit(solution)/shard_map/ppermute | solution.py:611
  50.6 2.2 %near.1 = (f32[2,8,1024]{2,1,0:T(8,128)S(1)}, f32[2,8,1024]{2,1,0:T(8,128)S(1)}, f32[2,128,1024]{2,1,0:T(8,128)S(1)}) custom-call(s32[4]{0:T(128)S(1)} %copy-done, s32[4,64]{1,0:T(4,128)S(1)} %copy-done.1, bf16[32,2,64,128]{3,2,1,0:T(8,128)(2,1)S(1)} %collective-permute-done.8.refs_2_, ...), custom_call_target="tpu_custom_call" | custom-call | flops 8589934592 | bytes 2097152 | tf_op jit(solution)/shard_map/near/pallas_call | solution.py:546
  52.8 1.7 %collective-permute-done.10.refs_3_ = bf16[16,2,64,128]{3,2,1,0:T(8,128)(2,1)S(1)} collective-permute-done((bf16[16,2,64,128]{3,2,1,0:T(8,128)(2,1)S(1)}, bf16[16,2,64,128]{3,2,1,0:T(8,128)(2,1)S(1)}, u32[]{:S(2)}, u32[]{:S(2)}) %collective-permute-start.10) | collective-permute-done | bytes 524320 | tf_op jit(solution)/shard_map/ppermute | solution.py:610
  54.6 4.5 %collective-permute-start.14 = (bf16[16,2,64,128]{3,2,1,0:T(8,128)(2,1)S(1)}, bf16[16,2,64,128]{3,2,1,0:T(8,128)(2,1)S(1)}, u32[]{:S(2)}, u32[]{:S(2)}) collective-permute-start(bf16[16,2,64,128]{3,2,1,0:T(8,128)(2,1)S(1)} %collective-permute-done.10.refs_3_), channel_id=1, source_target_pairs={{0,1},{1,0},{2,3},{3,2},{4,5},{5,4},{6,7},{7,6},{8,9},{9,8},{10,11... | collective-permute-start | bytes 1572872 | tf_op jit(solution)/shard_map/ppermute | solution.py:567
  59.1 9.7 %collective-permute-start.16 = (bf16[8,64,128]{2,1,0:T(8,128)(2,1)S(1)}, bf16[8,64,128]{2,1,0:T(8,128)(2,1)S(1)}, u32[]{:S(2)}, u32[]{:S(2)}) collective-permute-start(bf16[8,64,128]{2,1,0:T(8,128)(2,1)S(1)} %constant_dynamic-update-slice_fusion.5.refs_0_), channel_id=1, source_target_pairs={{0,32},{32,64},{64,96},{96,0},{1,33},{33,65},{65,97},{97,1},{2,34}... | collective-permute-start | bytes 393224 | tf_op jit(solution)/shard_map/ppermute | solution.py:617
  68.8 10.0 %collective-permute-start.17 = (bf16[8,64,128]{2,1,0:T(8,128)(2,1)S(1)}, bf16[8,64,128]{2,1,0:T(8,128)(2,1)S(1)}, u32[]{:S(2)}, u32[]{:S(2)}) collective-permute-start(bf16[8,64,128]{2,1,0:T(8,128)(2,1)S(1)} %constant_dynamic-update-slice_fusion.5.refs_0_), channel_id=1, source_target_pairs={{0,64},{32,96},{64,0},{96,32},{1,65},{33,97},{65,1},{97,33},{2,66}... | collective-permute-start | bytes 393224 | tf_op jit(solution)/shard_map/ppermute | solution.py:617
  78.8 6.8 %far.2 = bf16[128,1024]{1,0:T(8,128)(2,1)S(1)} custom-call(s32[4]{0:T(128)S(1)} %copy-done, s32[4,64]{1,0:T(4,128)S(1)} %copy-done.1, bf16[32,2,64,128]{3,2,1,0:T(8,128)(2,1)S(1)} %collective-permute-done.9.refs_2_, bf16[16,2,64,128]{3,2,1,0:T(8,128)(2,1)S(1)} %collective-permute-done.10.refs_3_, ...), custom_call_target="tpu_custom_call" | custom-call | flops 8589934592 | bytes 2097152 | tf_op jit(solution)/shard_map/far/pallas_call | solution.py:546
  85.7 6.6 %far.3 = bf16[128,1024]{1,0:T(8,128)(2,1)S(1)} custom-call(s32[4]{0:T(128)S(1)} %copy-done, s32[4,64]{1,0:T(4,128)S(1)} %copy-done.1, bf16[32,2,64,128]{3,2,1,0:T(8,128)(2,1)S(1)} %collective-permute-done.9.refs_2_, bf16[16,2,64,128]{3,2,1,0:T(8,128)(2,1)S(1)} %collective-permute-done.10.refs_3_, ...), custom_call_target="tpu_custom_call" | custom-call | flops 8589934592 | bytes 2097152 | tf_op jit(solution)/shard_map/far/pallas_call | solution.py:546
  92.5 4.2 %collective-permute-start.15 = (bf16[128,1024]{1,0:T(8,128)(2,1)S(1)}, bf16[128,1024]{1,0:T(8,128)(2,1)S(1)}, u32[]{:S(2)}, u32[]{:S(2)}) collective-permute-start(bf16[128,1024]{1,0:T(8,128)(2,1)S(1)} %far.2), channel_id=1, source_target_pairs={{0,0},{4,1},{2,2},{6,3},{1,4},{5,5},{3,6},{7,7},{8,8},{12,9},{10,1... | collective-permute-start | bytes 786440 | tf_op jit(solution)/shard_map/ppermute | solution.py:632
  96.7 3.1 %place.1 = bf16[2,6,64,512]{3,2,1,0:T(8,128)(2,1)} custom-call(s32[4]{0:T(128)} %hits.1, s32[4,16]{1,0:T(4,128)} %dests.1, bf16[2,6,64,512]{3,2,1,0:T(8,128)(2,1)} %cache.3, bf16[8,64,128]{2,1,0:T(8,128)(2,1)} %copy-done.2, bf16[8,64,128]{2,1,0:T(8,128)(2,1)} %copy-done.3, bf16[8,64,128]{2,1,0:T(8,128)(2,1)} %copy-done.4, bf16[8,64,128]{2,1,0:T(8,128)(2,1)} %copy-done.5), custom_call_target="tpu_custom_call" | custom-call | tf_op jit(solution)/shard_map/place/pallas_call | solution.py:165
  99.8 2.4 %collective-permute-done.19 = bf16[128,1024]{1,0:T(8,128)(2,1)S(1)} collective-permute-done((bf16[128,1024]{1,0:T(8,128)(2,1)S(1)}, bf16[128,1024]{1,0:T(8,128)(2,1)S(1)}, u32[]{:S(2)}, u32[]{:S(2)}) %collective-permute-start.19) | collective-permute-done | bytes 262176 | tf_op jit(solution)/shard_map/ppermute | solution.py:632
  102.3 0.9 maximum_select_fusion
  (44 shorter events, 0.5 us)
Async XLA Ops:
  2.7 13.4 %collective-permute-start.1 = (bf16[1280,128]{1,0:T(8,128)(2,1)}, bf16[1280,128]{1,0:T(8,128)(2,1)S(1)}, u32[]{:S(2)}, u32[]{:S(2)}) collective-permute-start(bf16[1280,128]{1,0:T(8,128)(2,1)} %get-tuple-element.44.after), channel_id=1, source_target_pairs={{0,2},{1,6},{2,0},{3,4},{4,3},{5,7},{6,1},{7,5},{8,10},{9,14},{10,... | collective-permute-start | bytes 983048 | tf_op jit(solution)/shard_map/ppermute | solution.py:584
  6.0 10.1 %collective-permute-start = (bf16[1280,128]{1,0:T(8,128)(2,1)}, bf16[1280,128]{1,0:T(8,128)(2,1)S(1)}, u32[]{:S(2)}, u32[]{:S(2)}) collective-permute-start(bf16[1280,128]{1,0:T(8,128)(2,1)} %get-tuple-element.45), channel_id=1, source_target_pairs={{0,0},{1,4},{2,2},{3,6},{4,1},{5,5},{6,3},{7,7},{8,8},{9,12},{10,1... | collective-permute-start | bytes 983048 | tf_op jit(solution)/shard_map/ppermute | solution.py:583
  10.8 15.8 %all-to-all-start = ((bf16[16,2,64,128]{3,2,1,0:T(8,128)(2,1)}), bf16[16,2,64,128]{3,2,1,0:T(8,128)(2,1)S(1)}, u32[]{:S(2)}, u32[]{:S(2)}) async-start(bf16[16,2,64,128]{3,2,1,0:T(8,128)(2,1)} %pack.1), calls=%async_computation | async-start | bytes 1048576 | tf_op jit(solution)/shard_map/all_to_all | solution.py:599
  16.1 6.1 %copy-start = (s32[4]{0:T(128)S(1)}, s32[4]{0:T(128)}, u32[]{:S(2)}) copy-start(s32[4]{0:T(128)} %hits.1) | copy-start | bytes 52
  16.2 6.1 %copy-start.1 = (s32[4,64]{1,0:T(4,128)S(1)}, s32[4,64]{1,0:T(4,128)}, u32[]{:S(2)}) copy-start(s32[4,64]{1,0:T(4,128)} %refs_1_.9) | copy-start | bytes 3076
  16.2 6.0 %collective-permute-start.2 = (bf16[4,2,64,128]{3,2,1,0:T(8,128)(2,1)S(1)}, bf16[4,2,64,128]{3,2,1,0:T(8,128)(2,1)S(1)}, u32[]{:S(2)}, u32[]{:S(2)}) collective-permute-start(bf16[4,2,64,128]{3,2,1,0:T(8,128)(2,1)S(1)} %pad_maximum_fusion.refs_2_.refs_3_), channel_id=1, source_target_pairs={{0,1},{1,0},{2,3},{3,2},{4,5},{5,4},{6,7},{7,6},{8,9},{9,8},{10,11... | collective-permute-start | bytes 393224 | tf_op jit(solution)/shard_map/ppermute | solution.py:567
  19.3 10.0 %collective-permute-start.4 = (bf16[4,2,64,128]{3,2,1,0:T(8,128)(2,1)S(1)}, bf16[4,2,64,128]{3,2,1,0:T(8,128)(2,1)S(1)}, u32[]{:S(2)}, u32[]{:S(2)}) collective-permute-start(bf16[4,2,64,128]{3,2,1,0:T(8,128)(2,1)S(1)} %pad_maximum_fusion.refs_2_.refs_3_), channel_id=1, source_target_pairs={{0,8},{8,16},{16,24},{24,0},{1,9},{9,17},{17,25},{25,1},{2,10},{10... | collective-permute-start | bytes 393224 | tf_op jit(solution)/shard_map/ppermute | solution.py:590
  20.2 9.1 %collective-permute-start.5 = (bf16[4,2,64,128]{3,2,1,0:T(8,128)(2,1)S(1)}, bf16[4,2,64,128]{3,2,1,0:T(8,128)(2,1)S(1)}, u32[]{:S(2)}, u32[]{:S(2)}) collective-permute-start(bf16[4,2,64,128]{3,2,1,0:T(8,128)(2,1)S(1)} %pad_maximum_fusion.refs_2_.refs_3_), channel_id=1, source_target_pairs={{0,24},{8,0},{16,8},{24,16},{1,25},{9,1},{17,9},{25,17},{2,26},{10... | collective-permute-start | bytes 393224 | tf_op jit(solution)/shard_map/ppermute | solution.py:590
  20.8 8.5 %collective-permute-start.6 = (bf16[4,2,64,128]{3,2,1,0:T(8,128)(2,1)S(1)}, bf16[4,2,64,128]{3,2,1,0:T(8,128)(2,1)S(1)}, u32[]{:S(2)}, u32[]{:S(2)}) collective-permute-start(bf16[4,2,64,128]{3,2,1,0:T(8,128)(2,1)S(1)} %pad_maximum_fusion.refs_2_.refs_3_), channel_id=1, source_target_pairs={{0,16},{8,24},{16,0},{24,8},{1,17},{9,25},{17,1},{25,9},{2,18},{10... | collective-permute-start | bytes 393224 | tf_op jit(solution)/shard_map/ppermute | solution.py:590
  26.6 4.2 %collective-permute-start.3 = (bf16[16,2,64,128]{3,2,1,0:T(8,128)(2,1)S(1)}, bf16[16,2,64,128]{3,2,1,0:T(8,128)(2,1)S(1)}, u32[]{:S(2)}, u32[]{:S(2)}) collective-permute-start(bf16[16,2,64,128]{3,2,1,0:T(8,128)(2,1)S(1)} %all-to-all-done), channel_id=1, source_target_pairs={{0,1},{1,0},{2,3},{3,2},{4,5},{5,4},{6,7},{7,6},{8,9},{9,8},{10,11... | collective-permute-start | bytes 1572872 | tf_op jit(solution)/shard_map/ppermute | solution.py:567
  29.4 2.0 %collective-permute-start.7 = (bf16[12,2,64,128]{3,2,1,0:T(8,128)(2,1)S(1)}, bf16[12,2,64,128]{3,2,1,0:T(8,128)(2,1)S(1)}, u32[]{:S(2)}, u32[]{:S(2)}) collective-permute-start(bf16[12,2,64,128]{3,2,1,0:T(8,128)(2,1)S(1)} %constant_dynamic-update-slice_fusion.2.refs_5_), channel_id=1, source_target_pairs={{0,1},{1,0},{2,3},{3,2},{4,5},{5,4},{6,7},{7,6},{8,9},{9,8},{10,11... | collective-permute-start | bytes 1179656 | tf_op jit(solution)/shard_map/ppermute | solution.py:567
  30.9 14.0 %collective-permute-start.8 = (bf16[32,2,64,128]{3,2,1,0:T(8,128)(2,1)S(1)}, bf16[32,2,64,128]{3,2,1,0:T(8,128)(2,1)S(1)}, u32[]{:S(2)}, u32[]{:S(2)}) collective-permute-start(bf16[32,2,64,128]{3,2,1,0:T(8,128)(2,1)S(1)} %constant_dynamic-update-slice_fusion.refs_2_), channel_id=1, source_target_pairs={{0,8},{1,25},{8,16},{9,1},{16,24},{17,9},{24,0},{25,17},{2,10},{3,... | collective-permute-start | bytes 3145736 | tf_op jit(solution)/shard_map/ppermute | solution.py:602
  44.9 33.9 %collective-permute-start.9 = (bf16[32,2,64,128]{3,2,1,0:T(8,128)(2,1)S(1)}, bf16[32,2,64,128]{3,2,1,0:T(8,128)(2,1)S(1)}, u32[]{:S(2)}, u32[]{:S(2)}) collective-permute-start(bf16[32,2,64,128]{3,2,1,0:T(8,128)(2,1)S(1)} %collective-permute-done.8.refs_2_), channel_id=1, source_target_pairs={{0,1},{1,0},{2,3},{3,2},{4,5},{5,4},{6,7},{7,6},{8,9},{9,8},{10,11... | collective-permute-start | bytes 3145736 | tf_op jit(solution)/shard_map/ppermute | solution.py:567
  46.2 8.4 %collective-permute-start.10 = (bf16[16,2,64,128]{3,2,1,0:T(8,128)(2,1)S(1)}, bf16[16,2,64,128]{3,2,1,0:T(8,128)(2,1)S(1)}, u32[]{:S(2)}, u32[]{:S(2)}) collective-permute-start(bf16[16,2,64,128]{3,2,1,0:T(8,128)(2,1)S(1)} %slice.11), channel_id=1, source_target_pairs={{0,8},{1,25},{8,16},{9,1},{16,24},{17,9},{24,0},{25,17},{2,10},{3,... | collective-permute-start | bytes 1572872 | tf_op jit(solution)/shard_map/ppermute | solution.py:610
  46.5 6.3 %collective-permute-start.11 = (bf16[2,64,128]{2,1,0:T(8,128)(2,1)S(1)}, bf16[2,64,128]{2,1,0:T(8,128)(2,1)S(1)}, u32[]{:S(2)}, u32[]{:S(2)}) collective-permute-start(bf16[2,64,128]{2,1,0:T(8,128)(2,1)S(1)} %get-tuple-element.68), channel_id=1, source_target_pairs={{0,2},{2,4},{4,6},{6,0},{1,3},{3,5},{5,7},{7,1},{8,10},{10,12},{12... | collective-permute-start | bytes 98312 | tf_op jit(solution)/shard_map/ppermute | solution.py:611
  47.0 5.8 %collective-permute-start.12 = (bf16[2,64,128]{2,1,0:T(8,128)(2,1)S(1)}, bf16[2,64,128]{2,1,0:T(8,128)(2,1)S(1)}, u32[]{:S(2)}, u32[]{:S(2)}) collective-permute-start(bf16[2,64,128]{2,1,0:T(8,128)(2,1)S(1)} %get-tuple-element.69), channel_id=1, source_target_pairs={{0,4},{2,6},{4,0},{6,2},{1,5},{3,7},{5,1},{7,3},{8,12},{10,14},{12... | collective-permute-start | bytes 98312 | tf_op jit(solution)/shard_map/ppermute | solution.py:611
  49.4 3.4 %collective-permute-start.13 = (bf16[2,64,128]{2,1,0:T(8,128)(2,1)S(1)}, bf16[2,64,128]{2,1,0:T(8,128)(2,1)S(1)}, u32[]{:S(2)}, u32[]{:S(2)}) collective-permute-start(bf16[2,64,128]{2,1,0:T(8,128)(2,1)S(1)} %get-tuple-element.70), channel_id=1, source_target_pairs={{0,6},{2,0},{4,2},{6,4},{1,7},{3,1},{5,3},{7,5},{8,14},{10,8},{12,... | collective-permute-start | bytes 98312 | tf_op jit(solution)/shard_map/ppermute | solution.py:611
  54.6 24.2 %collective-permute-start.14 = (bf16[16,2,64,128]{3,2,1,0:T(8,128)(2,1)S(1)}, bf16[16,2,64,128]{3,2,1,0:T(8,128)(2,1)S(1)}, u32[]{:S(2)}, u32[]{:S(2)}) collective-permute-start(bf16[16,2,64,128]{3,2,1,0:T(8,128)(2,1)S(1)} %collective-permute-done.10.refs_3_), channel_id=1, source_target_pairs={{0,1},{1,0},{2,3},{3,2},{4,5},{5,4},{6,7},{7,6},{8,9},{9,8},{10,11... | collective-permute-start | bytes 1572872 | tf_op jit(solution)/shard_map/ppermute | solution.py:567
  59.1 26.6 %copy-start.2 = (bf16[8,64,128]{2,1,0:T(8,128)(2,1)}, bf16[8,64,128]{2,1,0:T(8,128)(2,1)S(1)}, u32[]{:S(2)}) copy-start(bf16[8,64,128]{2,1,0:T(8,128)(2,1)S(1)} %constant_dynamic-update-slice_fusion.5.refs_0_) | copy-start | bytes 393220
  59.1 26.6 %collective-permute-start.16 = (bf16[8,64,128]{2,1,0:T(8,128)(2,1)S(1)}, bf16[8,64,128]{2,1,0:T(8,128)(2,1)S(1)}, u32[]{:S(2)}, u32[]{:S(2)}) collective-permute-start(bf16[8,64,128]{2,1,0:T(8,128)(2,1)S(1)} %constant_dynamic-update-slice_fusion.5.refs_0_), channel_id=1, source_target_pairs={{0,32},{32,64},{64,96},{96,0},{1,33},{33,65},{65,97},{97,1},{2,34}... | collective-permute-start | bytes 393224 | tf_op jit(solution)/shard_map/ppermute | solution.py:617
  68.8 16.9 %collective-permute-start.17 = (bf16[8,64,128]{2,1,0:T(8,128)(2,1)S(1)}, bf16[8,64,128]{2,1,0:T(8,128)(2,1)S(1)}, u32[]{:S(2)}, u32[]{:S(2)}) collective-permute-start(bf16[8,64,128]{2,1,0:T(8,128)(2,1)S(1)} %constant_dynamic-update-slice_fusion.5.refs_0_), channel_id=1, source_target_pairs={{0,64},{32,96},{64,0},{96,32},{1,65},{33,97},{65,1},{97,33},{2,66}... | collective-permute-start | bytes 393224 | tf_op jit(solution)/shard_map/ppermute | solution.py:617
  78.8 6.9 %collective-permute-start.18 = (bf16[8,64,128]{2,1,0:T(8,128)(2,1)S(1)}, bf16[8,64,128]{2,1,0:T(8,128)(2,1)S(1)}, u32[]{:S(2)}, u32[]{:S(2)}) collective-permute-start(bf16[8,64,128]{2,1,0:T(8,128)(2,1)S(1)} %constant_dynamic-update-slice_fusion.5.refs_0_), channel_id=1, source_target_pairs={{0,96},{32,0},{64,32},{96,64},{1,97},{33,1},{65,33},{97,65},{2,98}... | collective-permute-start | bytes 393224 | tf_op jit(solution)/shard_map/ppermute | solution.py:617
  85.7 6.7 %copy-start.3 = (bf16[8,64,128]{2,1,0:T(8,128)(2,1)}, bf16[8,64,128]{2,1,0:T(8,128)(2,1)S(1)}, u32[]{:S(2)}) copy-start(bf16[8,64,128]{2,1,0:T(8,128)(2,1)S(1)} %collective-permute-done.16.refs_1_) | copy-start | bytes 393220
  85.7 6.7 %copy-start.4 = (bf16[8,64,128]{2,1,0:T(8,128)(2,1)}, bf16[8,64,128]{2,1,0:T(8,128)(2,1)S(1)}, u32[]{:S(2)}) copy-start(bf16[8,64,128]{2,1,0:T(8,128)(2,1)S(1)} %collective-permute-done.17.refs_2_) | copy-start | bytes 393220
  85.7 6.7 %copy-start.5 = (bf16[8,64,128]{2,1,0:T(8,128)(2,1)}, bf16[8,64,128]{2,1,0:T(8,128)(2,1)S(1)}, u32[]{:S(2)}) copy-start(bf16[8,64,128]{2,1,0:T(8,128)(2,1)S(1)} %collective-permute-done.18.refs_3_) | copy-start | bytes 393220
  92.4 9.9 %collective-permute-start.19 = (bf16[128,1024]{1,0:T(8,128)(2,1)S(1)}, bf16[128,1024]{1,0:T(8,128)(2,1)S(1)}, u32[]{:S(2)}, u32[]{:S(2)}) collective-permute-start(bf16[128,1024]{1,0:T(8,128)(2,1)S(1)} %far.3), channel_id=1, source_target_pairs={{2,0},{6,1},{0,2},{4,3},{3,4},{7,5},{1,6},{5,7},{10,8},{14,9},{8,1... | collective-permute-start | bytes 786440 | tf_op jit(solution)/shard_map/ppermute | solution.py:632
  92.5 9.8 %collective-permute-start.15 = (bf16[128,1024]{1,0:T(8,128)(2,1)S(1)}, bf16[128,1024]{1,0:T(8,128)(2,1)S(1)}, u32[]{:S(2)}, u32[]{:S(2)}) collective-permute-start(bf16[128,1024]{1,0:T(8,128)(2,1)S(1)} %far.2), channel_id=1, source_target_pairs={{0,0},{4,1},{2,2},{6,3},{1,4},{5,5},{3,6},{7,7},{8,8},{12,9},{10,1... | collective-permute-start | bytes 786440 | tf_op jit(solution)/shard_map/ppermute | solution.py:632

commit v3 on v2

--- a/solution.py
+++ b/solution.py
@@ -168,7 +168,7 @@
         in_specs=[SMEM, SMEM, ANY] + [ANY] * 4,
         out_specs=ANY,
         scratch_shapes=[pltpu.VMEM(cache.shape, BF16), pltpu.SemaphoreType.DMA((22,))],
-        compiler_params=params(),
+        compiler_params=params(24),
         name="place",
     )(hits, dests, cache, *arrived)
 
@@ -555,8 +555,29 @@
     )(hits, table, *sources, *messages, *state)
 
 
-def by_parity(parity, even, odd):
-    return jnp.where(parity == 0, even, odd)
+def put_kernel(order, part, *refs):
+    out, sems = refs[-2:]
+    copies = Copies(sems)
+    start = pl.multiple_of((position()[2] + order) % 2 * ROWS, ROWS)
+    copies.start(part, out.at[0, :, pl.ds(start, ROWS)])
+    copies.wait()
+
+
+def put(order, part, into=None):
+    into = () if into is None else (into,)
+    return pl.pallas_call(
+        functools.partial(put_kernel, order),
+        out_shape=jax.ShapeDtypeStruct((1, HD, 2 * ROWS), BF16),
+        in_specs=[VMEM] + [ANY] * len(into),
+        out_specs=ANY,
+        scratch_shapes=[pltpu.SemaphoreType.DMA((1,))],
+        input_output_aliases={1: 0} if into else {},
+        compiler_params=params(12),
+        cost_estimate=pl.CostEstimate(
+            flops=1 if into else 10**10, bytes_accessed=1, transcendentals=0
+        ),
+        name="put",
+    )(part, *into)
 
 
 def shift(n, k):
@@ -572,7 +593,6 @@
 
 
 def shards(queries, suffix_kv, kv_cache, hits, table, dests):
-    parity = lax.axis_index("y") % 2
     msg_a, msg_b = make_messages(queries, suffix_kv)
     sent = pack(table, kv_cache, msg_b)
     to_a = [(y * 2 + c, (2 * c + y % 2) * 2 + y // 2) for y in range(4) for c in range(2)]
@@ -630,9 +650,7 @@
             arrived, state, _ = lax.optimization_barrier((arrived, state, out))
         (out,) = attend(hits, table, plan, None, 64, sources, messages, state, (r,), "far")
         outs.append(lax.ppermute(out, yc, back))
-    attended = by_parity(
-        parity, jnp.concatenate(outs, axis=1), jnp.concatenate(outs[::-1], axis=1)
-    )[None]
+    attended = put(1, outs[1], put(0, outs[0]))
     cache_out = place(hits, dests, kv_cache, arrived)
     return attended, cache_out
 

time: 105 us -> 103 us (0.981)
  the two profiles are of different devices: /device:TPU:5 before, /device:TPU:1 now
where the time goes in v3:
time: 103 us; the launch traced here: 105 us
  Pallas kernels  51.3 us (50%)
  starting transfers between devices  49.3 us (48%)
  waiting for transfers between devices  2.71 us (3%)
  between operations  1.16 us (1%)
    pallas_call x5, Pallas kernels, attend(): pl.pallas_call(functools.partial(attend_kernel, plan, early, len(sources)...  43 us
    ppermute x1, starting transfers between devices, shards(): far = lax.ppermute(got[:16], xc, ring)  12.7 us
    ppermute x5, starting transfers between devices, swap(): return lax.ppermute(part, 'c', shift(2, 1))  5.59 us
    all_to_all x1, starting transfers between devices, shards(): own = lax.all_to_all(sent, ('s', 'y'), 0, 0, tiled=True)  5.26 us
    ppermute x2, starting transfers between devices, shards(): outs.append(lax.ppermute(out, yc, back))  5.09 us
    ppermute x3, starting transfers between devices, shards(): lax.ppermute(parts[k], 'y', shift(4, k))  4.83 us
    ppermute x3, starting transfers between devices, shards(): rest = [lax.ppermute(fresh, 'x', shift(4, -k)) for k in NEIGHBOURS]  4.22 us
    ppermute x1, starting transfers between devices, shards(): msg_b = lax.ppermute(msg_b, yc, to_b)  4.2 us
  transfers between devices with their start and end apart: 21, of which 3 were waited for; matrix products, arithmetic and copies ran while one was open for 0% of the time, Pallas kernels for 46%

profile of v3, /device:TPU:1, one launch (start us, length us, event | category | flops | bytes accessed | tf_op | source)
XLA Modules:
  0.0 104.8 jit_solution(11911832924413567418)
XLA Ops:
  0.6 2.0 %messages.1 = (bf16[1280,128]{1,0:T(8,128)(2,1)}, bf16[1280,128]{1,0:T(8,128)(2,1)}) custom-call(bf16[1,128,2048]{2,1,0:T(8,128)(2,1)} %queries.1, bf16[2,1,128,256]{3,2,1,0:T(8,128)(2,1)} %suffix.1), custom_call_target="tpu_custom_call" | custom-call | tf_op jit(solution)/shard_map/messages/pallas_call | solution.py:84
  2.7 4.2 %collective-permute-start.1 = (bf16[1280,128]{1,0:T(8,128)(2,1)}, bf16[1280,128]{1,0:T(8,128)(2,1)S(1)}, u32[]{:S(2)}, u32[]{:S(2)}) collective-permute-start(bf16[1280,128]{1,0:T(8,128)(2,1)} %get-tuple-element.44.after), channel_id=1, source_target_pairs={{0,2},{1,6},{2,0},{3,4},{4,3},{5,7},{6,1},{7,5},{8,10},{9,14},{10,... | collective-permute-start | bytes 983048 | tf_op jit(solution)/shard_map/ppermute | solution.py:604
  6.9 2.1 %collective-permute-start = (bf16[1280,128]{1,0:T(8,128)(2,1)}, bf16[1280,128]{1,0:T(8,128)(2,1)S(1)}, u32[]{:S(2)}, u32[]{:S(2)}) collective-permute-start(bf16[1280,128]{1,0:T(8,128)(2,1)} %get-tuple-element.45), channel_id=1, source_target_pairs={{0,0},{1,4},{2,2},{3,6},{4,1},{5,5},{6,3},{7,7},{8,8},{9,12},{10,1... | collective-permute-start | bytes 983048 | tf_op jit(solution)/shard_map/ppermute | solution.py:603
  9.0 2.7 %pack.1 = bf16[16,2,64,128]{3,2,1,0:T(8,128)(2,1)} custom-call(s32[4,64]{1,0:T(4,128)} %refs_1_.9, bf16[2,6,64,512]{3,2,1,0:T(8,128)(2,1)} %cache.3, bf16[1280,128]{1,0:T(8,128)(2,1)} %get-tuple-element.44.after), custom_call_target="tpu_custom_call" | custom-call | flops 34359738368 | bytes 2097152 | tf_op jit(solution)/shard_map/pack/pallas_call | solution.py:122
  11.7 5.3 %all-to-all-start = ((bf16[16,2,64,128]{3,2,1,0:T(8,128)(2,1)}), bf16[16,2,64,128]{3,2,1,0:T(8,128)(2,1)S(1)}, u32[]{:S(2)}, u32[]{:S(2)}) async-start(bf16[16,2,64,128]{3,2,1,0:T(8,128)(2,1)} %pack.1), calls=%async_computation | async-start | bytes 1048576 | tf_op jit(solution)/shard_map/all_to_all | solution.py:619
  17.0 3.1 %collective-permute-start.2 = (bf16[4,2,64,128]{3,2,1,0:T(8,128)(2,1)S(1)}, bf16[4,2,64,128]{3,2,1,0:T(8,128)(2,1)S(1)}, u32[]{:S(2)}, u32[]{:S(2)}) collective-permute-start(bf16[4,2,64,128]{3,2,1,0:T(8,128)(2,1)S(1)} %pad_maximum_fusion.refs_2_.refs_3_), channel_id=1, source_target_pairs={{0,1},{1,0},{2,3},{3,2},{4,5},{5,4},{6,7},{7,6},{8,9},{9,8},{10,11... | collective-permute-start | bytes 393224 | tf_op jit(solution)/shard_map/ppermute | solution.py:588
  20.1 1.2 %collective-permute-start.4 = (bf16[4,2,64,128]{3,2,1,0:T(8,128)(2,1)S(1)}, bf16[4,2,64,128]{3,2,1,0:T(8,128)(2,1)S(1)}, u32[]{:S(2)}, u32[]{:S(2)}) collective-permute-start(bf16[4,2,64,128]{3,2,1,0:T(8,128)(2,1)S(1)} %pad_maximum_fusion.refs_2_.refs_3_), channel_id=1, source_target_pairs={{0,8},{8,16},{16,24},{24,0},{1,9},{9,17},{17,25},{25,1},{2,10},{10... | collective-permute-start | bytes 393224 | tf_op jit(solution)/shard_map/ppermute | solution.py:610
  21.4 1.5 %collective-permute-start.5 = (bf16[4,2,64,128]{3,2,1,0:T(8,128)(2,1)S(1)}, bf16[4,2,64,128]{3,2,1,0:T(8,128)(2,1)S(1)}, u32[]{:S(2)}, u32[]{:S(2)}) collective-permute-start(bf16[4,2,64,128]{3,2,1,0:T(8,128)(2,1)S(1)} %pad_maximum_fusion.refs_2_.refs_3_), channel_id=1, source_target_pairs={{0,24},{8,0},{16,8},{24,16},{1,25},{9,1},{17,9},{25,17},{2,26},{10... | collective-permute-start | bytes 393224 | tf_op jit(solution)/shard_map/ppermute | solution.py:610
  22.8 1.5 %collective-permute-start.6 = (bf16[4,2,64,128]{3,2,1,0:T(8,128)(2,1)S(1)}, bf16[4,2,64,128]{3,2,1,0:T(8,128)(2,1)S(1)}, u32[]{:S(2)}, u32[]{:S(2)}) collective-permute-start(bf16[4,2,64,128]{3,2,1,0:T(8,128)(2,1)S(1)} %pad_maximum_fusion.refs_2_.refs_3_), channel_id=1, source_target_pairs={{0,16},{8,24},{16,0},{24,8},{1,17},{9,25},{17,1},{25,9},{2,18},{10... | collective-permute-start | bytes 393224 | tf_op jit(solution)/shard_map/ppermute | solution.py:610
  24.4 4.4 %diagonal.1 = (f32[2,8,1024]{2,1,0:T(8,128)S(1)}, f32[2,8,1024]{2,1,0:T(8,128)S(1)}, f32[2,128,1024]{2,1,0:T(8,128)S(1)}) custom-call(s32[4]{0:T(128)S(1)} %copy-done.2, s32[4,64]{1,0:T(4,128)S(1)} %copy-done.3, bf16[4,2,64,128]{3,2,1,0:T(8,128)(2,1)S(1)} %pad_maximum_fusion.refs_2_.refs_3_, ...), custom_call_target="tpu_custom_call" | custom-call | flops 2147483648 | bytes 2097152 | tf_op jit(solution)/shard_map/diagonal/pallas_call | solution.py:546
  28.7 1.4 %collective-permute-start.3 = (bf16[16,2,64,128]{3,2,1,0:T(8,128)(2,1)S(1)}, bf16[16,2,64,128]{3,2,1,0:T(8,128)(2,1)S(1)}, u32[]{:S(2)}, u32[]{:S(2)}) collective-permute-start(bf16[16,2,64,128]{3,2,1,0:T(8,128)(2,1)S(1)} %all-to-all-done), channel_id=1, source_target_pairs={{0,1},{1,0},{2,3},{3,2},{4,5},{5,4},{6,7},{7,6},{8,9},{9,8},{10,11... | collective-permute-start | bytes 1572872 | tf_op jit(solution)/shard_map/ppermute | solution.py:588
  30.2 0.9 collective-permute-start.7
  31.2 0.4 collective-permute-done.3
  31.7 2.5 %collective-permute-start.8 = (bf16[32,2,64,128]{3,2,1,0:T(8,128)(2,1)S(1)}, bf16[32,2,64,128]{3,2,1,0:T(8,128)(2,1)S(1)}, u32[]{:S(2)}, u32[]{:S(2)}) collective-permute-start(bf16[32,2,64,128]{3,2,1,0:T(8,128)(2,1)S(1)} %constant_dynamic-update-slice_fusion.refs_2_), channel_id=1, source_target_pairs={{0,8},{1,25},{8,16},{9,1},{16,24},{17,9},{24,0},{25,17},{2,10},{3,... | collective-permute-start | bytes 3145736 | tf_op jit(solution)/shard_map/ppermute | solution.py:622
  34.3 17.2 %own.1 = (f32[2,8,1024]{2,1,0:T(8,128)S(1)}, f32[2,8,1024]{2,1,0:T(8,128)S(1)}, f32[2,128,1024]{2,1,0:T(8,128)S(1)}, bf16[2,64,128]{2,1,0:T(8,128)(2,1)S(1)}, bf...) custom-call(s32[4]{0:T(128)S(1)} %copy-done.2, ...), custom_call_target="tpu_custom_call" | custom-call | flops 15032385536 | bytes 2097152 | tf_op jit(solution)/shard_map/own/pallas_call | solution.py:546
  51.5 0.1 collective-permute-start.9
  51.7 12.7 %collective-permute-start.10 = (bf16[16,2,64,128]{3,2,1,0:T(8,128)(2,1)S(1)}, bf16[16,2,64,128]{3,2,1,0:T(8,128)(2,1)S(1)}, u32[]{:S(2)}, u32[]{:S(2)}) collective-permute-start(bf16[16,2,64,128]{3,2,1,0:T(8,128)(2,1)S(1)} %slice.11), channel_id=1, source_target_pairs={{0,8},{1,25},{8,16},{9,1},{16,24},{17,9},{24,0},{25,17},{2,10},{3,... | collective-permute-start | bytes 1572872 | tf_op jit(solution)/shard_map/ppermute | solution.py:630
  64.4 1.3 %collective-permute-start.11 = (bf16[2,64,128]{2,1,0:T(8,128)(2,1)S(1)}, bf16[2,64,128]{2,1,0:T(8,128)(2,1)S(1)}, u32[]{:S(2)}, u32[]{:S(2)}) collective-permute-start(bf16[2,64,128]{2,1,0:T(8,128)(2,1)S(1)} %get-tuple-element.68), channel_id=1, source_target_pairs={{0,2},{2,4},{4,6},{6,0},{1,3},{3,5},{5,7},{7,1},{8,10},{10,12},{12... | collective-permute-start | bytes 98312 | tf_op jit(solution)/shard_map/ppermute | solution.py:631
  65.7 2.4 %collective-permute-start.12 = (bf16[2,64,128]{2,1,0:T(8,128)(2,1)S(1)}, bf16[2,64,128]{2,1,0:T(8,128)(2,1)S(1)}, u32[]{:S(2)}, u32[]{:S(2)}) collective-permute-start(bf16[2,64,128]{2,1,0:T(8,128)(2,1)S(1)} %get-tuple-element.69), channel_id=1, source_target_pairs={{0,4},{2,6},{4,0},{6,2},{1,5},{3,7},{5,1},{7,3},{8,12},{10,14},{12... | collective-permute-start | bytes 98312 | tf_op jit(solution)/shard_map/ppermute | solution.py:631
  68.1 1.2 %collective-permute-start.13 = (bf16[2,64,128]{2,1,0:T(8,128)(2,1)S(1)}, bf16[2,64,128]{2,1,0:T(8,128)(2,1)S(1)}, u32[]{:S(2)}, u32[]{:S(2)}) collective-permute-start(bf16[2,64,128]{2,1,0:T(8,128)(2,1)S(1)} %get-tuple-element.70), channel_id=1, source_target_pairs={{0,6},{2,0},{4,2},{6,4},{1,7},{3,1},{5,3},{7,5},{8,14},{10,8},{12,... | collective-permute-start | bytes 98312 | tf_op jit(solution)/shard_map/ppermute | solution.py:631
  69.2 7.2 %near.1 = (f32[2,8,1024]{2,1,0:T(8,128)S(1)}, f32[2,8,1024]{2,1,0:T(8,128)S(1)}, f32[2,128,1024]{2,1,0:T(8,128)S(1)}) custom-call(s32[4]{0:T(128)S(1)} %copy-done.2, s32[4,64]{1,0:T(4,128)S(1)} %copy-done.3, bf16[32,2,64,128]{3,2,1,0:T(8,128)(2,1)S(1)} %collective-permute-done.8.refs_2_, ...), custom_call_target="tpu_custom_call" | custom-call | flops 8589934592 | bytes 2097152 | tf_op jit(solution)/shard_map/near/pallas_call | solution.py:546
  76.5 0.1 collective-permute-start.14
  76.8 0.1 collective-permute-start.16
  76.9 2.6 %collective-permute-start.17 = (bf16[8,64,128]{2,1,0:T(8,128)(2,1)S(1)}, bf16[8,64,128]{2,1,0:T(8,128)(2,1)S(1)}, u32[]{:S(2)}, u32[]{:S(2)}) collective-permute-start(bf16[8,64,128]{2,1,0:T(8,128)(2,1)S(1)} %constant_dynamic-update-slice_fusion.5.refs_0_), channel_id=1, source_target_pairs={{0,96},{32,0},{64,32},{96,64},{1,97},{33,1},{65,33},{97,65},{2,98}... | collective-permute-start | bytes 393224 | tf_op jit(solution)/shard_map/ppermute | solution.py:637
  79.4 7.2 %far.2 = bf16[128,1024]{1,0:T(8,128)(2,1)S(1)} custom-call(s32[4]{0:T(128)S(1)} %copy-done.2, s32[4,64]{1,0:T(4,128)S(1)} %copy-done.3, bf16[32,2,64,128]{3,2,1,0:T(8,128)(2,1)S(1)} %collective-permute-done.9.refs_2_, bf16[16,2,64,128]{3,2,1,0:T(8,128)(2,1)S(1)} %collective-permute-done.10.refs_3_, ...), custom_call_target="tpu_custom_call" | custom-call | flops 8589934592 | bytes 2097152 | tf_op jit(solution)/shard_map/far/pallas_call | solution.py:546
  86.6 3.2 %collective-permute-start.19 = (bf16[128,1024]{1,0:T(8,128)(2,1)S(1)}, bf16[128,1024]{1,0:T(8,128)(2,1)S(1)}, u32[]{:S(2)}, u32[]{:S(2)}) collective-permute-start(bf16[128,1024]{1,0:T(8,128)(2,1)S(1)} %far.2), channel_id=1, source_target_pairs={{0,0},{4,1},{2,2},{6,3},{1,4},{5,5},{3,6},{7,7},{8,8},{12,9},{10,1... | collective-permute-start | bytes 786440 | tf_op jit(solution)/shard_map/ppermute | solution.py:652
  89.9 7.0 %far.3 = bf16[128,1024]{1,0:T(8,128)(2,1)S(1)} custom-call(s32[4]{0:T(128)S(1)} %copy-done.2, s32[4,64]{1,0:T(4,128)S(1)} %copy-done.3, bf16[32,2,64,128]{3,2,1,0:T(8,128)(2,1)S(1)} %collective-permute-done.9.refs_2_, bf16[16,2,64,128]{3,2,1,0:T(8,128)(2,1)S(1)} %collective-permute-done.10.refs_3_, ...), custom_call_target="tpu_custom_call" | custom-call | flops 8589934592 | bytes 2097152 | tf_op jit(solution)/shard_map/far/pallas_call | solution.py:546
  96.8 1.9 %collective-permute-start.18 = (bf16[128,1024]{1,0:T(8,128)(2,1)S(1)}, bf16[128,1024]{1,0:T(8,128)(2,1)S(1)}, u32[]{:S(2)}, u32[]{:S(2)}) collective-permute-start(bf16[128,1024]{1,0:T(8,128)(2,1)S(1)} %far.3), channel_id=1, source_target_pairs={{2,0},{6,1},{0,2},{4,3},{3,4},{7,5},{1,6},{5,7},{10,8},{14,9},{8,1... | collective-permute-start | bytes 786440 | tf_op jit(solution)/shard_map/ppermute | solution.py:652
  98.7 2.2 %place.1 = bf16[2,6,64,512]{3,2,1,0:T(8,128)(2,1)} custom-call(s32[4]{0:T(128)S(1)} %copy-done.2, s32[4,16]{1,0:T(4,128)S(1)} %copy-done.1, bf16[2,6,64,512]{3,2,1,0:T(8,128)(2,1)S(1)} %copy-done, bf16[8,64,128]{2,1,0:T(8,128)(2,1)S(1)} %constant_dynamic-update-slice_fusion.5.refs_0_, bf16[8,64,128]{2,1,0:T(8,128)(2,1)S(1)} %collective-permute-done.15.refs_1_, ...), custom_call_target="tpu_custom_call" | custom-call | tf_op jit(solution)/shard_map/place/pallas_call | solution.py:165
  101.0 0.7 put.2.refs_0_
  101.7 2.2 %collective-permute-done.18.part = bf16[128,1024]{1,0:T(8,128)(2,1)S(1)} collective-permute-done((bf16[128,1024]{1,0:T(8,128)(2,1)S(1)}, bf16[128,1024]{1,0:T(8,128)(2,1)S(1)}, u32[]{:S(2)}, u32[]{:S(2)}) %collective-permute-start.18) | collective-permute-done | bytes 262176 | tf_op jit(solution)/shard_map/ppermute | solution.py:652
  103.9 0.7 put.3
  (41 shorter events, 0.5 us)
Async XLA Ops:
  2.7 14.3 %collective-permute-start.1 = (bf16[1280,128]{1,0:T(8,128)(2,1)}, bf16[1280,128]{1,0:T(8,128)(2,1)S(1)}, u32[]{:S(2)}, u32[]{:S(2)}) collective-permute-start(bf16[1280,128]{1,0:T(8,128)(2,1)} %get-tuple-element.44.after), channel_id=1, source_target_pairs={{0,2},{1,6},{2,0},{3,4},{4,3},{5,7},{6,1},{7,5},{8,10},{9,14},{10,... | collective-permute-start | bytes 983048 | tf_op jit(solution)/shard_map/ppermute | solution.py:604
  6.9 10.1 %collective-permute-start = (bf16[1280,128]{1,0:T(8,128)(2,1)}, bf16[1280,128]{1,0:T(8,128)(2,1)S(1)}, u32[]{:S(2)}, u32[]{:S(2)}) collective-permute-start(bf16[1280,128]{1,0:T(8,128)(2,1)} %get-tuple-element.45), channel_id=1, source_target_pairs={{0,0},{1,4},{2,2},{3,6},{4,1},{5,5},{6,3},{7,7},{8,8},{9,12},{10,1... | collective-permute-start | bytes 983048 | tf_op jit(solution)/shard_map/ppermute | solution.py:603
  11.7 17.1 %all-to-all-start = ((bf16[16,2,64,128]{3,2,1,0:T(8,128)(2,1)}), bf16[16,2,64,128]{3,2,1,0:T(8,128)(2,1)S(1)}, u32[]{:S(2)}, u32[]{:S(2)}) async-start(bf16[16,2,64,128]{3,2,1,0:T(8,128)(2,1)} %pack.1), calls=%async_computation | async-start | bytes 1048576 | tf_op jit(solution)/shard_map/all_to_all | solution.py:619
  17.0 7.4 %copy-start.2 = (s32[4]{0:T(128)S(1)}, s32[4]{0:T(128)}, u32[]{:S(2)}) copy-start(s32[4]{0:T(128)} %hits.1) | copy-start | bytes 52
  17.0 7.4 %copy-start.3 = (s32[4,64]{1,0:T(4,128)S(1)}, s32[4,64]{1,0:T(4,128)}, u32[]{:S(2)}) copy-start(s32[4,64]{1,0:T(4,128)} %refs_1_.9) | copy-start | bytes 3076
  17.0 7.4 %collective-permute-start.2 = (bf16[4,2,64,128]{3,2,1,0:T(8,128)(2,1)S(1)}, bf16[4,2,64,128]{3,2,1,0:T(8,128)(2,1)S(1)}, u32[]{:S(2)}, u32[]{:S(2)}) collective-permute-start(bf16[4,2,64,128]{3,2,1,0:T(8,128)(2,1)S(1)} %pad_maximum_fusion.refs_2_.refs_3_), channel_id=1, source_target_pairs={{0,1},{1,0},{2,3},{3,2},{4,5},{5,4},{6,7},{7,6},{8,9},{9,8},{10,11... | collective-permute-start | bytes 393224 | tf_op jit(solution)/shard_map/ppermute | solution.py:588
  20.1 10.0 %collective-permute-start.4 = (bf16[4,2,64,128]{3,2,1,0:T(8,128)(2,1)S(1)}, bf16[4,2,64,128]{3,2,1,0:T(8,128)(2,1)S(1)}, u32[]{:S(2)}, u32[]{:S(2)}) collective-permute-start(bf16[4,2,64,128]{3,2,1,0:T(8,128)(2,1)S(1)} %pad_maximum_fusion.refs_2_.refs_3_), channel_id=1, source_target_pairs={{0,8},{8,16},{16,24},{24,0},{1,9},{9,17},{17,25},{25,1},{2,10},{10... | collective-permute-start | bytes 393224 | tf_op jit(solution)/shard_map/ppermute | solution.py:610
  21.4 8.8 %collective-permute-start.5 = (bf16[4,2,64,128]{3,2,1,0:T(8,128)(2,1)S(1)}, bf16[4,2,64,128]{3,2,1,0:T(8,128)(2,1)S(1)}, u32[]{:S(2)}, u32[]{:S(2)}) collective-permute-start(bf16[4,2,64,128]{3,2,1,0:T(8,128)(2,1)S(1)} %pad_maximum_fusion.refs_2_.refs_3_), channel_id=1, source_target_pairs={{0,24},{8,0},{16,8},{24,16},{1,25},{9,1},{17,9},{25,17},{2,26},{10... | collective-permute-start | bytes 393224 | tf_op jit(solution)/shard_map/ppermute | solution.py:610
  22.8 7.4 %collective-permute-start.6 = (bf16[4,2,64,128]{3,2,1,0:T(8,128)(2,1)S(1)}, bf16[4,2,64,128]{3,2,1,0:T(8,128)(2,1)S(1)}, u32[]{:S(2)}, u32[]{:S(2)}) collective-permute-start(bf16[4,2,64,128]{3,2,1,0:T(8,128)(2,1)S(1)} %pad_maximum_fusion.refs_2_.refs_3_), channel_id=1, source_target_pairs={{0,16},{8,24},{16,0},{24,8},{1,17},{9,25},{17,1},{25,9},{2,18},{10... | collective-permute-start | bytes 393224 | tf_op jit(solution)/shard_map/ppermute | solution.py:610
  28.7 2.9 %collective-permute-start.3 = (bf16[16,2,64,128]{3,2,1,0:T(8,128)(2,1)S(1)}, bf16[16,2,64,128]{3,2,1,0:T(8,128)(2,1)S(1)}, u32[]{:S(2)}, u32[]{:S(2)}) collective-permute-start(bf16[16,2,64,128]{3,2,1,0:T(8,128)(2,1)S(1)} %all-to-all-done), channel_id=1, source_target_pairs={{0,1},{1,0},{2,3},{3,2},{4,5},{5,4},{6,7},{7,6},{8,9},{9,8},{10,11... | collective-permute-start | bytes 1572872 | tf_op jit(solution)/shard_map/ppermute | solution.py:588
  30.2 4.0 %collective-permute-start.7 = (bf16[12,2,64,128]{3,2,1,0:T(8,128)(2,1)S(1)}, bf16[12,2,64,128]{3,2,1,0:T(8,128)(2,1)S(1)}, u32[]{:S(2)}, u32[]{:S(2)}) collective-permute-start(bf16[12,2,64,128]{3,2,1,0:T(8,128)(2,1)S(1)} %constant_dynamic-update-slice_fusion.2.refs_5_), channel_id=1, source_target_pairs={{0,1},{1,0},{2,3},{3,2},{4,5},{5,4},{6,7},{7,6},{8,9},{9,8},{10,11... | collective-permute-start | bytes 1179656 | tf_op jit(solution)/shard_map/ppermute | solution.py:588
  31.7 19.8 %collective-permute-start.8 = (bf16[32,2,64,128]{3,2,1,0:T(8,128)(2,1)S(1)}, bf16[32,2,64,128]{3,2,1,0:T(8,128)(2,1)S(1)}, u32[]{:S(2)}, u32[]{:S(2)}) collective-permute-start(bf16[32,2,64,128]{3,2,1,0:T(8,128)(2,1)S(1)} %constant_dynamic-update-slice_fusion.refs_2_), channel_id=1, source_target_pairs={{0,8},{1,25},{8,16},{9,1},{16,24},{17,9},{24,0},{25,17},{2,10},{3,... | collective-permute-start | bytes 3145736 | tf_op jit(solution)/shard_map/ppermute | solution.py:622
  51.5 27.9 %collective-permute-start.9 = (bf16[32,2,64,128]{3,2,1,0:T(8,128)(2,1)S(1)}, bf16[32,2,64,128]{3,2,1,0:T(8,128)(2,1)S(1)}, u32[]{:S(2)}, u32[]{:S(2)}) collective-permute-start(bf16[32,2,64,128]{3,2,1,0:T(8,128)(2,1)S(1)} %collective-permute-done.8.refs_2_), channel_id=1, source_target_pairs={{0,1},{1,0},{2,3},{3,2},{4,5},{5,4},{6,7},{7,6},{8,9},{9,8},{10,11... | collective-permute-start | bytes 3145736 | tf_op jit(solution)/shard_map/ppermute | solution.py:588
  51.7 24.8 %collective-permute-start.10 = (bf16[16,2,64,128]{3,2,1,0:T(8,128)(2,1)S(1)}, bf16[16,2,64,128]{3,2,1,0:T(8,128)(2,1)S(1)}, u32[]{:S(2)}, u32[]{:S(2)}) collective-permute-start(bf16[16,2,64,128]{3,2,1,0:T(8,128)(2,1)S(1)} %slice.11), channel_id=1, source_target_pairs={{0,8},{1,25},{8,16},{9,1},{16,24},{17,9},{24,0},{25,17},{2,10},{3,... | collective-permute-start | bytes 1572872 | tf_op jit(solution)/shard_map/ppermute | solution.py:630
  64.4 12.1 %collective-permute-start.11 = (bf16[2,64,128]{2,1,0:T(8,128)(2,1)S(1)}, bf16[2,64,128]{2,1,0:T(8,128)(2,1)S(1)}, u32[]{:S(2)}, u32[]{:S(2)}) collective-permute-start(bf16[2,64,128]{2,1,0:T(8,128)(2,1)S(1)} %get-tuple-element.68), channel_id=1, source_target_pairs={{0,2},{2,4},{4,6},{6,0},{1,3},{3,5},{5,7},{7,1},{8,10},{10,12},{12... | collective-permute-start | bytes 98312 | tf_op jit(solution)/shard_map/ppermute | solution.py:631
  65.7 10.8 %collective-permute-start.12 = (bf16[2,64,128]{2,1,0:T(8,128)(2,1)S(1)}, bf16[2,64,128]{2,1,0:T(8,128)(2,1)S(1)}, u32[]{:S(2)}, u32[]{:S(2)}) collective-permute-start(bf16[2,64,128]{2,1,0:T(8,128)(2,1)S(1)} %get-tuple-element.69), channel_id=1, source_target_pairs={{0,4},{2,6},{4,0},{6,2},{1,5},{3,7},{5,1},{7,3},{8,12},{10,14},{12... | collective-permute-start | bytes 98312 | tf_op jit(solution)/shard_map/ppermute | solution.py:631
  68.1 8.4 %collective-permute-start.13 = (bf16[2,64,128]{2,1,0:T(8,128)(2,1)S(1)}, bf16[2,64,128]{2,1,0:T(8,128)(2,1)S(1)}, u32[]{:S(2)}, u32[]{:S(2)}) collective-permute-start(bf16[2,64,128]{2,1,0:T(8,128)(2,1)S(1)} %get-tuple-element.70), channel_id=1, source_target_pairs={{0,6},{2,0},{4,2},{6,4},{1,7},{3,1},{5,3},{7,5},{8,14},{10,8},{12,... | collective-permute-start | bytes 98312 | tf_op jit(solution)/shard_map/ppermute | solution.py:631
  76.5 2.9 %collective-permute-start.14 = (bf16[16,2,64,128]{3,2,1,0:T(8,128)(2,1)S(1)}, bf16[16,2,64,128]{3,2,1,0:T(8,128)(2,1)S(1)}, u32[]{:S(2)}, u32[]{:S(2)}) collective-permute-start(bf16[16,2,64,128]{3,2,1,0:T(8,128)(2,1)S(1)} %collective-permute-done.10.refs_3_), channel_id=1, source_target_pairs={{0,1},{1,0},{2,3},{3,2},{4,5},{5,4},{6,7},{7,6},{8,9},{9,8},{10,11... | collective-permute-start | bytes 1572872 | tf_op jit(solution)/shard_map/ppermute | solution.py:588
  76.7 13.2 %collective-permute-start.15 = (bf16[8,64,128]{2,1,0:T(8,128)(2,1)S(1)}, bf16[8,64,128]{2,1,0:T(8,128)(2,1)S(1)}, u32[]{:S(2)}, u32[]{:S(2)}) collective-permute-start(bf16[8,64,128]{2,1,0:T(8,128)(2,1)S(1)} %constant_dynamic-update-slice_fusion.5.refs_0_), channel_id=1, source_target_pairs={{0,32},{32,64},{64,96},{96,0},{1,33},{33,65},{65,97},{97,1},{2,34}... | collective-permute-start | bytes 393224 | tf_op jit(solution)/shard_map/ppermute | solution.py:637
  76.8 13.1 %collective-permute-start.16 = (bf16[8,64,128]{2,1,0:T(8,128)(2,1)S(1)}, bf16[8,64,128]{2,1,0:T(8,128)(2,1)S(1)}, u32[]{:S(2)}, u32[]{:S(2)}) collective-permute-start(bf16[8,64,128]{2,1,0:T(8,128)(2,1)S(1)} %constant_dynamic-update-slice_fusion.5.refs_0_), channel_id=1, source_target_pairs={{0,64},{32,96},{64,0},{96,32},{1,65},{33,97},{65,1},{97,33},{2,66}... | collective-permute-start | bytes 393224 | tf_op jit(solution)/shard_map/ppermute | solution.py:637
  76.9 13.0 %collective-permute-start.17 = (bf16[8,64,128]{2,1,0:T(8,128)(2,1)S(1)}, bf16[8,64,128]{2,1,0:T(8,128)(2,1)S(1)}, u32[]{:S(2)}, u32[]{:S(2)}) collective-permute-start(bf16[8,64,128]{2,1,0:T(8,128)(2,1)S(1)} %constant_dynamic-update-slice_fusion.5.refs_0_), channel_id=1, source_target_pairs={{0,96},{32,0},{64,32},{96,64},{1,97},{33,1},{65,33},{97,65},{2,98}... | collective-permute-start | bytes 393224 | tf_op jit(solution)/shard_map/ppermute | solution.py:637
  86.6 12.1 %copy-start = (bf16[2,6,64,512]{3,2,1,0:T(8,128)(2,1)S(1)}, bf16[2,6,64,512]{3,2,1,0:T(8,128)(2,1)}, u32[]{:S(2)}) copy-start(bf16[2,6,64,512]{3,2,1,0:T(8,128)(2,1)} %cache.3) | copy-start | bytes 2359300
  86.6 12.1 %copy-start.1 = (s32[4,16]{1,0:T(4,128)S(1)}, s32[4,16]{1,0:T(4,128)}, u32[]{:S(2)}) copy-start(s32[4,16]{1,0:T(4,128)} %dests.1) | copy-start | bytes 772
  86.6 14.4 %collective-permute-start.19 = (bf16[128,1024]{1,0:T(8,128)(2,1)S(1)}, bf16[128,1024]{1,0:T(8,128)(2,1)S(1)}, u32[]{:S(2)}, u32[]{:S(2)}) collective-permute-start(bf16[128,1024]{1,0:T(8,128)(2,1)S(1)} %far.2), channel_id=1, source_target_pairs={{0,0},{4,1},{2,2},{6,3},{1,4},{5,5},{3,6},{7,7},{8,8},{12,9},{10,1... | collective-permute-start | bytes 786440 | tf_op jit(solution)/shard_map/ppermute | solution.py:652
  96.8 7.1 %collective-permute-start.18 = (bf16[128,1024]{1,0:T(8,128)(2,1)S(1)}, bf16[128,1024]{1,0:T(8,128)(2,1)S(1)}, u32[]{:S(2)}, u32[]{:S(2)}) collective-permute-start(bf16[128,1024]{1,0:T(8,128)(2,1)S(1)} %far.3), channel_id=1, source_target_pairs={{2,0},{6,1},{0,2},{4,3},{3,4},{7,5},{1,6},{5,7},{10,8},{14,9},{8,1... | collective-permute-start | bytes 786440 | tf_op jit(solution)/shard_map/ppermute | solution.py:652
